TPU v7x, 32 devices: a whole 2x2x4 slice. The times are simulated.
32 devices in a mesh: frame: 2 (over y), space: 8 (over z, x), dp: 2 (over core).
Axes of the slice: x: 2, y: 2, z: 4, core: 2. Of those that a mesh axis runs over, the one named last changes fastest.
Arguments:
- frames_in: bfloat16 [4, 1024, 768], P(('dp', 'frame'), 'space'), parts along dimension 0, may hold values from -6 to 6
- cotangent: bfloat16 [4, 1024, 768], P(('dp', 'frame'), 'space'), parts along dimension 0, may hold values from -6 to 6
- w_qkv_space: bfloat16 [768, 2304], P('space'), may hold values from -0.21875 to 0.21875
- w_out_space: bfloat16 [768, 768], P('space'), may hold values from -0.875 to 0.875
- w_qkv_time: bfloat16 [768, 2304], P('space'), may hold values from -0.21875 to 0.21875
- w_out_time: bfloat16 [768, 768], P('space'), may hold values from -0.21875 to 0.21875
- neighbours: int32 [8, 4], replicated, may hold values from 0 to 7, as said below
Outputs:
- frames_out: bfloat16 [4, 1024, 768], P(('dp', 'frame'), 'space'), parts along dimension 0
- grad_frames: bfloat16 [4, 1024, 768], P(('dp', 'frame'), 'space'), parts along dimension 0
There are 2 independent parts, one for each index of `dp`. A program takes and returns all parts, laid end to end along the dimension named above; an argument that names none is the same for every part. Nothing has to cross between parts.
Inputs may be any that keep to these rules, and one draw needn't show every extreme that they name: `neighbours`: row b lists block b first; every entry c satisfies |c - b| <= 1; entries may repeat, and a repeated entry counts once.
All inputs are finite; a program needn't handle non-finite values.
Results may differ from a plain program's by a relative error of at most 0.023.
Values may be sent and summed in bfloat16 or wider, within the bound.
A program may use at most 64 MiB of HBM per device.

v0:
```python
import jax
import jax.numpy as jnp
from jax import lax
from jax.sharding import PartitionSpec as P

HEADS = 12
HD = 64
BLOCK = 128


EPS = 1e-06


def padded(cells, sides, width):
    for axis, dim in sides:
        count = lax.axis_size(axis)
        ends = count - 1
        head = lax.slice_in_dim(cells, 0, width, axis=dim)
        tail = lax.slice_in_dim(cells, cells.shape[dim] - width, cells.shape[dim], axis=dim)
        cells = jnp.concatenate(
            [
                lax.ppermute(tail, axis, [(i, (i + 1) % count) for i in range(ends)]),
                cells,
                lax.ppermute(head, axis, [((i + 1) % count, i) for i in range(ends)]),
            ],
            axis=dim,
        )
    return cells


def rms_norm(row_data):
    values = row_data.astype(jnp.float32)
    factor = lax.rsqrt(jnp.mean(values * values, axis=-1, keepdims=True) + EPS)
    return (values * factor).astype(jnp.bfloat16)


def rms_back(row_data, upstream):
    values = row_data.astype(jnp.float32)
    factor = lax.rsqrt(jnp.mean(values * values, axis=-1, keepdims=True) + EPS)
    inner_mean = jnp.mean(values * upstream, axis=-1, keepdims=True)
    return factor * upstream - values * factor**3 * inner_mean


def block_mask(neighbour_rows, first_id):
    block_count = neighbour_rows.shape[0]
    candidate = first_id + jnp.arange(3 * block_count, dtype=jnp.int32)
    matches = jnp.any(neighbour_rows[:, :, None] == candidate[None, None, :], axis=1)
    return jnp.repeat(jnp.repeat(matches, BLOCK, axis=0), BLOCK, axis=1)


def space_attend(queries, key_rows, value_rows, allowed):
    score_scale = HD ** (-0.5)
    query_count = queries.shape[0]
    key_count = key_rows.shape[0]
    output_list = []
    total_list = []
    for head_pair in range(HEADS // 2):
        start_col = head_pair * 2 * HD
        stop_col = start_col + 2 * HD
        query_part = queries[:, start_col:stop_col].reshape(query_count, 2, HD)
        key_part = key_rows[:, start_col:stop_col].reshape(key_count, 2, HD)
        value_part = value_rows[:, start_col:stop_col].reshape(key_count, 2, HD)
        scores = (
            jnp.einsum("sgh,tgh->gst", query_part, key_part, preferred_element_type=jnp.float32)
            * score_scale
        )
        exponent = jnp.where(allowed[None], jnp.exp(scores), 0.0)
        totals = jnp.sum(exponent, axis=-1)
        probability = (exponent / totals[:, :, None]).astype(jnp.bfloat16)
        combined = jnp.einsum(
            "gst,tgh->sgh", probability, value_part, preferred_element_type=jnp.float32
        )
        output_list.append(combined.astype(jnp.bfloat16).reshape(query_count, 2 * HD))
        total_list.append(totals)
    return (jnp.concatenate(output_list, axis=1), jnp.concatenate(total_list, axis=0))


def space_back(queries, key_rows, value_rows, allowed, totals, attended, grad_attended):
    score_scale = HD ** (-0.5)
    query_count = queries.shape[0]
    key_count = key_rows.shape[0]
    query_list = []
    key_list = []
    value_list = []
    for head_pair in range(HEADS // 2):
        start_col = head_pair * 2 * HD
        stop_col = start_col + 2 * HD
        query_part = queries[:, start_col:stop_col].reshape(query_count, 2, HD)
        key_part = key_rows[:, start_col:stop_col].reshape(key_count, 2, HD)
        value_part = value_rows[:, start_col:stop_col].reshape(key_count, 2, HD)
        out_part = attended[:, start_col:stop_col].reshape(query_count, 2, HD)
        grad_part = grad_attended[:, start_col:stop_col].reshape(query_count, 2, HD)
        scores = (
            jnp.einsum("sgh,tgh->gst", query_part, key_part, preferred_element_type=jnp.float32)
            * score_scale
        )
        exponent = jnp.where(allowed[None], jnp.exp(scores), 0.0)
        weight = exponent / totals[2 * head_pair : 2 * head_pair + 2, :, None]
        probability = weight.astype(jnp.bfloat16)
        prob_grad = jnp.einsum(
            "sgh,tgh->gst", grad_part, value_part, preferred_element_type=jnp.float32
        )
        row_delta = jnp.einsum(
            "sgh,sgh->gs", grad_part, out_part, preferred_element_type=jnp.float32
        )
        score_grad = (weight * (prob_grad - row_delta[:, :, None])).astype(jnp.bfloat16)
        query_grad = (
            jnp.einsum("gst,tgh->sgh", score_grad, key_part, preferred_element_type=jnp.float32)
            * score_scale
        )
        key_grad = (
            jnp.einsum("gst,sgh->tgh", score_grad, query_part, preferred_element_type=jnp.float32)
            * score_scale
        )
        value_grad = jnp.einsum(
            "gst,sgh->tgh", probability, grad_part, preferred_element_type=jnp.float32
        )
        query_list.append(query_grad.astype(jnp.bfloat16).reshape(query_count, 2 * HD))
        key_list.append(key_grad.reshape(key_count, 2 * HD))
        value_list.append(value_grad.reshape(key_count, 2 * HD))
    return (
        jnp.concatenate(query_list, axis=1),
        jnp.concatenate(key_list, axis=1),
        jnp.concatenate(value_list, axis=1),
    )


def time_attend(queries, key_rows, value_rows):
    frame_count, position_count, feature_count = queries.shape
    split_shape = (frame_count, position_count, HEADS, HD)
    score_scale = HD ** (-0.5)
    scores = (
        jnp.einsum(
            "fphd,gphd->phfg",
            queries.reshape(split_shape),
            key_rows.reshape(split_shape),
            preferred_element_type=jnp.float32,
        )
        * score_scale
    )
    causal = jnp.arange(frame_count)[:, None] >= jnp.arange(frame_count)[None, :]
    exponent = jnp.where(causal, jnp.exp(scores), 0.0)
    totals = jnp.sum(exponent, axis=-1)
    probability = (exponent / totals[..., None]).astype(jnp.bfloat16)
    combined = jnp.einsum(
        "phfg,gphd->fphd",
        probability,
        value_rows.reshape(split_shape),
        preferred_element_type=jnp.float32,
    )
    return (
        combined.astype(jnp.bfloat16).reshape(frame_count, position_count, feature_count),
        totals,
    )


def time_back(queries, key_rows, value_rows, attended, grad_attended, totals):
    frame_count, position_count, feature_count = queries.shape
    split_shape = (frame_count, position_count, HEADS, HD)
    score_scale = HD ** (-0.5)
    query_four = queries.reshape(split_shape)
    key_four = key_rows.reshape(split_shape)
    value_four = value_rows.reshape(split_shape)
    out_four = attended.reshape(split_shape)
    grad_four = grad_attended.reshape(split_shape)
    scores = (
        jnp.einsum("fphd,gphd->phfg", query_four, key_four, preferred_element_type=jnp.float32)
        * score_scale
    )
    causal = jnp.arange(frame_count)[:, None] >= jnp.arange(frame_count)[None, :]
    exponent = jnp.where(causal, jnp.exp(scores), 0.0)
    weight = exponent / totals[..., None]
    probability = weight.astype(jnp.bfloat16)
    prob_grad = jnp.einsum(
        "fphd,gphd->phfg", grad_four, value_four, preferred_element_type=jnp.float32
    )
    row_delta = jnp.einsum(
        "fphd,fphd->phf", grad_four, out_four, preferred_element_type=jnp.float32
    )
    score_grad = (weight * (prob_grad - row_delta[..., None])).astype(jnp.bfloat16)
    query_grad = (
        jnp.einsum("phfg,gphd->fphd", score_grad, key_four, preferred_element_type=jnp.float32)
        * score_scale
    )
    key_grad = (
        jnp.einsum("phfg,fphd->gphd", score_grad, query_four, preferred_element_type=jnp.float32)
        * score_scale
    )
    value_grad = jnp.einsum(
        "phfg,fphd->gphd", probability, grad_four, preferred_element_type=jnp.float32
    )
    pieces = [
        gradient.astype(jnp.bfloat16).reshape(frame_count, position_count, feature_count)
        for gradient in (query_grad, key_grad, value_grad)
    ]
    return jnp.concatenate(pieces, axis=-1)


def to_frames(local_rows):
    return lax.all_to_all(local_rows[None], "frame", split_axis=1, concat_axis=0, tiled=True)


def to_space(frame_rows):
    return lax.all_to_all(frame_rows, "frame", split_axis=0, concat_axis=1, tiled=True)[0]


def rim(first_part, second_part, width):
    return (padded(first_part, (("space", 0),), width), padded(second_part, (("space", 0),), width))


def local(frames_in, cotangent, w_qkv_space, w_out_space, w_qkv_time, w_out_time, neighbours):
    local_in = frames_in[0]
    grad_out = cotangent[0]
    shard, feature_count = local_in.shape
    full_qkv_space, full_out_space, full_qkv_time, full_out_time = (
        lax.all_gather(w_qkv_space, "space", axis=0, tiled=True),
        lax.all_gather(w_out_space, "space", axis=0, tiled=True),
        lax.all_gather(w_qkv_time, "space", axis=0, tiled=True),
        lax.all_gather(w_out_time, "space", axis=0, tiled=True),
    )
    block_count = shard // BLOCK
    space_index = lax.axis_index("space")
    lists_here = lax.dynamic_slice_in_dim(neighbours, space_index * block_count, block_count, 0)
    allowed = block_mask(lists_here, (space_index - 1) * block_count)
    normed_space = rms_norm(local_in)
    projected = jnp.dot(normed_space, full_qkv_space, preferred_element_type=jnp.float32).astype(
        jnp.bfloat16
    )
    queries = projected[:, :feature_count]
    key_window, value_window = rim(
        projected[:, feature_count : 2 * feature_count], projected[:, 2 * feature_count :], shard
    )
    attended, totals = space_attend(queries, key_window, value_window, allowed)
    update = jnp.dot(attended, full_out_space, preferred_element_type=jnp.float32)
    stream = (local_in.astype(jnp.float32) + update).astype(jnp.bfloat16)
    normed_time = rms_norm(stream)
    projected_time = jnp.dot(normed_time, full_qkv_time, preferred_element_type=jnp.float32).astype(
        jnp.bfloat16
    )
    time_rows = to_frames(projected_time)
    query_time = time_rows[..., :feature_count]
    key_time = time_rows[..., feature_count : 2 * feature_count]
    value_time = time_rows[..., 2 * feature_count :]
    attended_time, totals_time = time_attend(query_time, key_time, value_time)
    attended_back = to_space(attended_time)
    update_time = jnp.dot(attended_back, full_out_time, preferred_element_type=jnp.float32)
    frames_out = (stream.astype(jnp.float32) + update_time).astype(jnp.bfloat16)
    grad_att_time = jnp.dot(grad_out, full_out_time.T, preferred_element_type=jnp.float32).astype(
        jnp.bfloat16
    )
    grad_time_rows = to_frames(grad_att_time)
    gradients = time_back(
        query_time, key_time, value_time, attended_time, grad_time_rows, totals_time
    )
    grad_project_time = to_space(gradients)
    grad_normed_time = jnp.dot(
        grad_project_time, full_qkv_time.T, preferred_element_type=jnp.float32
    )
    grad_stream = (grad_out.astype(jnp.float32) + rms_back(stream, grad_normed_time)).astype(
        jnp.bfloat16
    )
    grad_attended = jnp.dot(
        grad_stream, full_out_space.T, preferred_element_type=jnp.float32
    ).astype(jnp.bfloat16)
    grad_query, key_partial, value_partial = space_back(
        queries, key_window, value_window, allowed, totals, attended, grad_attended
    )
    key_send = jnp.concatenate([key_partial[:shard], key_partial[2 * shard :]], axis=0).astype(
        jnp.bfloat16
    )
    value_send = jnp.concatenate(
        [value_partial[:shard], value_partial[2 * shard :]], axis=0
    ).astype(jnp.bfloat16)
    key_got, value_got = rim(key_send, value_send, shard)
    grad_key = (
        key_partial[shard : 2 * shard]
        + key_got[:shard].astype(jnp.float32)
        + key_got[3 * shard :].astype(jnp.float32)
    ).astype(jnp.bfloat16)
    grad_value = (
        value_partial[shard : 2 * shard]
        + value_got[:shard].astype(jnp.float32)
        + value_got[3 * shard :].astype(jnp.float32)
    ).astype(jnp.bfloat16)
    grad_project = jnp.concatenate([grad_query, grad_key, grad_value], axis=1)
    grad_normed = jnp.dot(grad_project, full_qkv_space.T, preferred_element_type=jnp.float32)
    grad_in = (grad_stream.astype(jnp.float32) + rms_back(local_in, grad_normed)).astype(
        jnp.bfloat16
    )
    return (frames_out[None], grad_in[None])


def solution(mesh):
    in_specs = (
        P(("dp", "frame"), "space", None),
        P(("dp", "frame"), "space", None),
        P("space", None),
        P("space", None),
        P("space", None),
        P("space", None),
        P(),
    )
    out_specs = (P(("dp", "frame"), "space", None), P(("dp", "frame"), "space", None))
    return jax.shard_map(local, mesh=mesh, in_specs=in_specs, out_specs=out_specs, check_vma=False)
```

profile of v0, /device:TPU:3, one launch (start us, length us, event | category | flops | bytes accessed | tf_op | source)
XLA Modules:
  0.0 334.2 jit_solution(651202734307975974)
XLA Ops:
  11.1 39.2 %all-gather.11.cloned.1.call-done = bf16[768,768]{1,0:T(8,128)(2,1)} async-done(((bf16[96,768]{1,0:T(8,128)(2,1)}), bf16[768,768]{1,0:T(8,128)(2,1)}) %all-gather.11.cloned.1.call-update) | async-done | bytes 1179664 | tf_op jit(solution)/shard_map/all_gather | solution.py:219
  50.3 1.8 fusion.33
  53.0 1.8 reduce.17
  55.6 3.4 %all-to-all-start.2 = ((bf16[2,2,24576]{2,1,0:T(2,128)(2,1)}), bf16[2,2,24576]{2,1,0:T(2,128)(2,1)S(1)}, u32[]{:S(2)}, u32[]{:S(2)}) async-start(bf16[2,2,24576]{2,1,0:T(2,128)(2,1)} %reshape.404), calls=%async_computation.2 | async-start | bytes 393216 | tf_op jit(solution)/shard_map/all_to_all | solution.py:200
  59.0 3.6 %all-to-all-done.2 = bf16[2,2,24576]{2,1,0:T(2,128)(2,1)S(1)} async-done(((bf16[2,2,24576]{2,1,0:T(2,128)(2,1)}), bf16[2,2,24576]{2,1,0:T(2,128)(2,1)S(1)}, u32[]{:S(2)}, u32[]{:S(2)}) %all-to-all-start.2) | async-done | bytes 196640 | tf_op jit(solution)/shard_map/all_to_all | solution.py:200
  65.5 51.4 %all-gather.5.cloned.1.call-done = bf16[768,2304]{1,0:T(8,128)(2,1)} async-done(((bf16[96,2304]{1,0:T(8,128)(2,1)}), bf16[768,2304]{1,0:T(8,128)(2,1)}) %all-gather.5.cloned.1.call-update) | async-done | bytes 3538960 | tf_op jit(solution)/shard_map/all_gather | solution.py:216
  116.8 2.7 convolution_convert_fusion.1
  119.5 3.5 %collective-permute-start.2 = (bf16[128,768]{1,0:T(8,128)(2,1)S(1)}, bf16[128,768]{1,0:T(8,128)(2,1)S(1)}, u32[]{:S(2)}, u32[]{:S(2)}) collective-permute-start(bf16[128,768]{1,0:T(8,128)(2,1)S(1)} %get-tuple-element.29), channel_id=1, source_target_pairs={{0,2},{2,4},{4,6},{6,8},{8,10},{10,12},{12,14},{1,3},{3,5},{5,7},{... | collective-permute-start | bytes 589832 | tf_op jit(solution)/shard_map/ppermute | solution.py:22
  123.0 1.9 collective-permute-start.3
  124.9 4.3 %collective-permute-start = (bf16[128,768]{1,0:T(8,128)(2,1)S(1)}, bf16[128,768]{1,0:T(8,128)(2,1)S(1)}, u32[]{:S(2)}, u32[]{:S(2)}) collective-permute-start(bf16[128,768]{1,0:T(8,128)(2,1)S(1)} %get-tuple-element.30), channel_id=1, source_target_pairs={{0,2},{2,4},{4,6},{6,8},{8,10},{10,12},{12,14},{1,3},{3,5},{5,7},{... | collective-permute-start | bytes 589832 | tf_op jit(solution)/shard_map/ppermute | solution.py:22
  129.2 2.1 collective-permute-start.1
  132.4 9.9 %collective-permute-done = bf16[128,768]{1,0:T(8,128)(2,1)S(1)} collective-permute-done((bf16[128,768]{1,0:T(8,128)(2,1)S(1)}, bf16[128,768]{1,0:T(8,128)(2,1)S(1)}, u32[]{:S(2)}, u32[]{:S(2)}) %collective-permute-start) | collective-permute-done | bytes 196640 | tf_op jit(solution)/shard_map/ppermute | solution.py:22
  147.8 18.0 %all-gather.7.cloned.1.call-done = bf16[768,768]{1,0:T(8,128)(2,1)} async-done(((bf16[96,768]{1,0:T(8,128)(2,1)}), bf16[768,768]{1,0:T(8,128)(2,1)}) %all-gather.7.cloned.1.call-update) | async-done | bytes 1179664 | tf_op jit(solution)/shard_map/all_gather | solution.py:217
  165.8 1.7 multiply_reduce_fusion.2
  171.6 60.6 %all-gather.9.cloned.1.call-done = bf16[768,2304]{1,0:T(8,128)(2,1)} async-done(((bf16[96,2304]{1,0:T(8,128)(2,1)}), bf16[768,2304]{1,0:T(8,128)(2,1)}) %all-gather.9.cloned.1.call-update) | async-done | bytes 3538960 | tf_op jit(solution)/shard_map/all_gather | solution.py:218
  232.2 2.7 fusion
  235.8 4.4 %reduce.18 = bf16[128,2304]{1,0:T(8,128)(2,1)S(1)} reduce(bf16[128,1,2304]{2,1,0:T(2,128)(2,1)S(1)} %bitcast.296, bf16[]{:T(256)} %broadcast.215), dimensions={1}, to_apply=%bitcast.294.reduce_sub_computation | reduce | bytes 1179650
  241.1 3.7 %all-to-all-start = ((bf16[2,2,73728]{2,1,0:T(2,128)(2,1)}), bf16[2,2,73728]{2,1,0:T(2,128)(2,1)S(1)}, u32[]{:S(2)}, u32[]{:S(2)}) async-start(bf16[2,2,73728]{2,1,0:T(2,128)(2,1)} %reshape.402), calls=%async_computation | async-start | bytes 1179648 | tf_op jit(solution)/shard_map/all_to_all | solution.py:200
  247.1 4.6 %all-to-all-done = bf16[2,2,73728]{2,1,0:T(2,128)(2,1)S(1)} async-done(((bf16[2,2,73728]{2,1,0:T(2,128)(2,1)}), bf16[2,2,73728]{2,1,0:T(2,128)(2,1)S(1)}, u32[]{:S(2)}, u32[]{:S(2)}) %all-to-all-start) | async-done | bytes 589856 | tf_op jit(solution)/shard_map/all_to_all | solution.py:200
  256.0 3.6 %multiply_reduce_fusion = (f32[64,12,2]{2,1,0:T(8,128)}, bf16[64,12,64,2]{2,3,1,0:T(2,128)(2,1)S(1)}) fusion(f32[64,12,2,64]{3,2,1,0:T(2,128)S(1)} %copy.278, bf16[64,12,2,2]{2,3,1,0:T(2,128)(2,1)} %copy.265, bf16[2,64,12,64]{3,2,1,0:T(8,128)(2,1)S(1)} %reshape.347), kind=kOutput, calls=%fused_computation.85 | convolution fusion | flops 784896 | bytes 798720 | tf_op jit(solution)/shard_map/phfg,gphd->fphd/dot_general | solution.py:145
  260.9 2.1 fusion.72
  269.5 3.4 %all-to-all-start.1 = ((bf16[2,64,768]{2,1,0:T(8,128)(2,1)}), bf16[2,64,768]{2,1,0:T(8,128)(2,1)S(1)}, u32[]{:S(2)}, u32[]{:S(2)}) async-start(bf16[2,64,768]{2,1,0:T(8,128)(2,1)} %reshape.350), calls=%async_computation.1 | async-start | bytes 393216 | tf_op jit(solution)/shard_map/all_to_all | solution.py:204
  273.8 2.8 all-to-all-done.1
  277.2 4.5 %all-to-all-start.3 = ((bf16[2,64,2304]{2,1,0:T(8,128)(2,1)}), bf16[2,64,2304]{2,1,0:T(8,128)(2,1)}, u32[]{:S(2)}, u32[]{:S(2)}) async-start(bf16[2,64,2304]{2,1,0:T(8,128)(2,1)} %pad_maximum_fusion.2), calls=%async_computation.3 | async-start | bytes 1179648 | tf_op jit(solution)/shard_map/all_to_all | solution.py:204
  281.8 2.2 fusion.60
  283.9 2.4 fusion.34
  287.4 2.6 multiply_reduce_fusion.1
  306.0 3.1 collective-permute-start.6
  309.1 2.1 collective-permute-start.7
  311.5 4.3 %collective-permute-start.4 = (bf16[128,768]{0,1:T(8,128)(2,1)S(1)}, bf16[128,768]{0,1:T(8,128)(2,1)S(1)}, u32[]{:S(2)}, u32[]{:S(2)}) collective-permute-start(bf16[128,768]{0,1:T(8,128)(2,1)S(1)} %get-tuple-element.6), channel_id=1, source_target_pairs={{0,2},{2,4},{4,6},{6,8},{8,10},{10,12},{12,14},{1,3},{3,5},{5,7},{... | collective-permute-start | bytes 589832 | tf_op jit(solution)/shard_map/ppermute | solution.py:22
  315.9 1.9 collective-permute-start.5
  317.9 7.3 %collective-permute-done.4 = bf16[128,768]{0,1:T(8,128)(2,1)S(1)} collective-permute-done((bf16[128,768]{0,1:T(8,128)(2,1)S(1)}, bf16[128,768]{0,1:T(8,128)(2,1)S(1)}, u32[]{:S(2)}, u32[]{:S(2)}) %collective-permute-start.4) | collective-permute-done | bytes 196640 | tf_op jit(solution)/shard_map/ppermute | solution.py:22
  (327 shorter events, 54.6 us)
Async XLA Ops:
  7.2 43.1 %copy-start.20 = (bf16[1,128,768]{2,1,0:T(8,128)(2,1)S(1)}, bf16[1,128,768]{2,1,0:T(8,128)(2,1)}, u32[]{:S(2)}) copy-start(bf16[1,128,768]{2,1,0:T(8,128)(2,1)} %param.8) | copy-start | bytes 589828
  7.2 43.1 %all-gather.11.cloned.1.call-start = ((), (), s32[]{:S(2)}) async-start(), calls=%async_computation.7 | async-start | bytes 1327104 | tf_op jit(solution)/shard_map/all_gather | solution.py:219
  7.9 108.9 %all-gather.5.cloned.1.call-start = ((), (), s32[]{:S(2)}) async-start(), calls=%async_computation.4 | async-start | bytes 3981312 | tf_op jit(solution)/shard_map/all_gather | solution.py:216
  8.7 157.1 %all-gather.7.cloned.1.call-start = ((), (), s32[]{:S(2)}) async-start(), calls=%async_computation.5 | async-start | bytes 1327104 | tf_op jit(solution)/shard_map/all_gather | solution.py:217
  9.4 222.7 %all-gather.9.cloned.1.call-start = ((), (), s32[]{:S(2)}) async-start(), calls=%async_computation.6 | async-start | bytes 3981312 | tf_op jit(solution)/shard_map/all_gather | solution.py:218
  55.6 7.1 %all-to-all-start.2 = ((bf16[2,2,24576]{2,1,0:T(2,128)(2,1)}), bf16[2,2,24576]{2,1,0:T(2,128)(2,1)S(1)}, u32[]{:S(2)}, u32[]{:S(2)}) async-start(bf16[2,2,24576]{2,1,0:T(2,128)(2,1)} %reshape.404), calls=%async_computation.2 | async-start | bytes 393216 | tf_op jit(solution)/shard_map/all_to_all | solution.py:200
  119.5 12.6 %collective-permute-start.2 = (bf16[128,768]{1,0:T(8,128)(2,1)S(1)}, bf16[128,768]{1,0:T(8,128)(2,1)S(1)}, u32[]{:S(2)}, u32[]{:S(2)}) collective-permute-start(bf16[128,768]{1,0:T(8,128)(2,1)S(1)} %get-tuple-element.29), channel_id=1, source_target_pairs={{0,2},{2,4},{4,6},{6,8},{8,10},{10,12},{12,14},{1,3},{3,5},{5,7},{... | collective-permute-start | bytes 589832 | tf_op jit(solution)/shard_map/ppermute | solution.py:22
  123.0 9.1 %collective-permute-start.3 = (bf16[128,768]{1,0:T(8,128)(2,1)S(1)}, bf16[128,768]{1,0:T(8,128)(2,1)S(1)}, u32[]{:S(2)}, u32[]{:S(2)}) collective-permute-start(bf16[128,768]{1,0:T(8,128)(2,1)S(1)} %get-tuple-element.29), channel_id=1, source_target_pairs={{2,0},{4,2},{6,4},{8,6},{10,8},{12,10},{14,12},{3,1},{5,3},{7,5},{... | collective-permute-start | bytes 589832 | tf_op jit(solution)/shard_map/ppermute | solution.py:24
  124.9 17.4 %collective-permute-start = (bf16[128,768]{1,0:T(8,128)(2,1)S(1)}, bf16[128,768]{1,0:T(8,128)(2,1)S(1)}, u32[]{:S(2)}, u32[]{:S(2)}) collective-permute-start(bf16[128,768]{1,0:T(8,128)(2,1)S(1)} %get-tuple-element.30), channel_id=1, source_target_pairs={{0,2},{2,4},{4,6},{6,8},{8,10},{10,12},{12,14},{1,3},{3,5},{5,7},{... | collective-permute-start | bytes 589832 | tf_op jit(solution)/shard_map/ppermute | solution.py:22
  129.2 13.1 %collective-permute-start.1 = (bf16[128,768]{1,0:T(8,128)(2,1)S(1)}, bf16[128,768]{1,0:T(8,128)(2,1)S(1)}, u32[]{:S(2)}, u32[]{:S(2)}) collective-permute-start(bf16[128,768]{1,0:T(8,128)(2,1)S(1)} %get-tuple-element.30), channel_id=1, source_target_pairs={{2,0},{4,2},{6,4},{8,6},{10,8},{12,10},{14,12},{3,1},{5,3},{7,5},{... | collective-permute-start | bytes 589832 | tf_op jit(solution)/shard_map/ppermute | solution.py:24
  131.5 36.7 %copy-start.52 = (bf16[128,128]{0,1:T(8,128)(2,1)}, bf16[128,128]{0,1:T(8,128)(2,1)S(1)}, u32[]{:S(2)}) copy-start(bf16[128,128]{0,1:T(8,128)(2,1)S(1)} %copy.232) | copy-start | bytes 98308
  131.6 37.7 %copy-start.50 = (bf16[128,128]{0,1:T(8,128)(2,1)}, bf16[128,128]{0,1:T(8,128)(2,1)S(1)}, u32[]{:S(2)}) copy-start(bf16[128,128]{0,1:T(8,128)(2,1)S(1)} %copy.229) | copy-start | bytes 98308
  131.7 38.7 %copy-start.54 = (bf16[128,128]{0,1:T(8,128)(2,1)}, bf16[128,128]{0,1:T(8,128)(2,1)S(1)}, u32[]{:S(2)}) copy-start(bf16[128,128]{0,1:T(8,128)(2,1)S(1)} %copy.235) | copy-start | bytes 98308
  131.9 112.9 %copy-start.56 = (bf16[128,128]{0,1:T(8,128)(2,1)}, bf16[128,128]{0,1:T(8,128)(2,1)S(1)}, u32[]{:S(2)}) copy-start(bf16[128,128]{0,1:T(8,128)(2,1)S(1)} %copy.238) | copy-start | bytes 98308
  132.0 114.0 %copy-start.58 = (bf16[128,128]{0,1:T(8,128)(2,1)}, bf16[128,128]{0,1:T(8,128)(2,1)S(1)}, u32[]{:S(2)}) copy-start(bf16[128,128]{0,1:T(8,128)(2,1)S(1)} %copy.241) | copy-start | bytes 98308
  132.1 15.1 %copy-start.60 = (bf16[128,128]{0,1:T(8,128)(2,1)}, bf16[128,128]{0,1:T(8,128)(2,1)S(1)}, u32[]{:S(2)}) copy-start(bf16[128,128]{0,1:T(8,128)(2,1)S(1)} %copy.244) | copy-start | bytes 98308
  132.4 35.8 %copy-start.8 = (bf16[384,128]{0,1:T(8,128)(2,1)}, bf16[384,128]{0,1:T(8,128)(2,1)S(1)}, u32[]{:S(2)}) copy-start(bf16[384,128]{0,1:T(8,128)(2,1)S(1)} %copy.233) | copy-start | bytes 294916
  142.8 26.5 %copy-start.10 = (bf16[384,128]{0,1:T(8,128)(2,1)}, bf16[384,128]{0,1:T(8,128)(2,1)S(1)}, u32[]{:S(2)}) copy-start(bf16[384,128]{0,1:T(8,128)(2,1)S(1)} %copy.230) | copy-start | bytes 294916
  143.0 27.4 %copy-start.12 = (bf16[384,128]{0,1:T(8,128)(2,1)}, bf16[384,128]{0,1:T(8,128)(2,1)S(1)}, u32[]{:S(2)}) copy-start(bf16[384,128]{0,1:T(8,128)(2,1)S(1)} %copy.236) | copy-start | bytes 294916
  143.3 101.5 %copy-start.14 = (bf16[384,128]{0,1:T(8,128)(2,1)}, bf16[384,128]{0,1:T(8,128)(2,1)S(1)}, u32[]{:S(2)}) copy-start(bf16[384,128]{0,1:T(8,128)(2,1)S(1)} %copy.239) | copy-start | bytes 294916
  143.6 102.3 %copy-start.16 = (bf16[384,128]{0,1:T(8,128)(2,1)}, bf16[384,128]{0,1:T(8,128)(2,1)S(1)}, u32[]{:S(2)}) copy-start(bf16[384,128]{0,1:T(8,128)(2,1)S(1)} %copy.242) | copy-start | bytes 294916
  147.1 20.4 %copy-start.70 = (bf16[2,64,128]{2,1,0:T(8,128)(2,1)}, bf16[2,64,128]{2,1,0:T(8,128)(2,1)S(1)}, u32[]{:S(2)}) copy-start(bf16[2,64,128]{2,1,0:T(8,128)(2,1)S(1)} %convolution_convert_fusion.7) | copy-start | bytes 98308
  147.5 20.1 %copy-start.30 = (f32[2,128,384]{2,1,0:T(8,128)}, f32[2,128,384]{2,1,0:T(8,128)S(1)}, u32[]{:S(2)}) copy-start(f32[2,128,384]{2,1,0:T(8,128)S(1)} %fusion.17) | copy-start | bytes 1179652
  147.8 21.5 %copy-start.72 = (bf16[2,64,128]{2,1,0:T(8,128)(2,1)}, bf16[2,64,128]{2,1,0:T(8,128)(2,1)S(1)}, u32[]{:S(2)}) copy-start(bf16[2,64,128]{2,1,0:T(8,128)(2,1)S(1)} %convolution_convert_fusion.6) | copy-start | bytes 98308
  167.6 64.6 %copy-start.3 = (f32[128,768]{1,0:T(8,128)}, f32[128,768]{1,0:T(8,128)S(1)}, u32[]{:S(2)}) copy-start(f32[128,768]{1,0:T(8,128)S(1)} %get-tuple-element.42) | copy-start | bytes 1179652
  241.1 10.6 %all-to-all-start = ((bf16[2,2,73728]{2,1,0:T(2,128)(2,1)}), bf16[2,2,73728]{2,1,0:T(2,128)(2,1)S(1)}, u32[]{:S(2)}, u32[]{:S(2)}) async-start(bf16[2,2,73728]{2,1,0:T(2,128)(2,1)} %reshape.402), calls=%async_computation | async-start | bytes 1179648 | tf_op jit(solution)/shard_map/all_to_all | solution.py:200
  269.5 7.1 %all-to-all-start.1 = ((bf16[2,64,768]{2,1,0:T(8,128)(2,1)}), bf16[2,64,768]{2,1,0:T(8,128)(2,1)S(1)}, u32[]{:S(2)}, u32[]{:S(2)}) async-start(bf16[2,64,768]{2,1,0:T(8,128)(2,1)} %reshape.350), calls=%async_computation.1 | async-start | bytes 393216 | tf_op jit(solution)/shard_map/all_to_all | solution.py:204
  277.2 10.1 %all-to-all-start.3 = ((bf16[2,64,2304]{2,1,0:T(8,128)(2,1)}), bf16[2,64,2304]{2,1,0:T(8,128)(2,1)}, u32[]{:S(2)}, u32[]{:S(2)}) async-start(bf16[2,64,2304]{2,1,0:T(8,128)(2,1)} %pad_maximum_fusion.2), calls=%async_computation.3 | async-start | bytes 1179648 | tf_op jit(solution)/shard_map/all_to_all | solution.py:204
  306.0 19.3 %collective-permute-start.6 = (bf16[128,768]{0,1:T(8,128)(2,1)S(1)}, bf16[128,768]{0,1:T(8,128)(2,1)S(1)}, u32[]{:S(2)}, u32[]{:S(2)}) collective-permute-start(bf16[128,768]{0,1:T(8,128)(2,1)S(1)} %get-tuple-element.4), channel_id=1, source_target_pairs={{0,2},{2,4},{4,6},{6,8},{8,10},{10,12},{12,14},{1,3},{3,5},{5,7},{... | collective-permute-start | bytes 589832 | tf_op jit(solution)/shard_map/ppermute | solution.py:22
  309.1 16.2 %collective-permute-start.7 = (bf16[128,768]{0,1:T(8,128)(2,1)S(1)}, bf16[128,768]{0,1:T(8,128)(2,1)S(1)}, u32[]{:S(2)}, u32[]{:S(2)}) collective-permute-start(bf16[128,768]{0,1:T(8,128)(2,1)S(1)} %get-tuple-element.5), channel_id=1, source_target_pairs={{2,0},{4,2},{6,4},{8,6},{10,8},{12,10},{14,12},{3,1},{5,3},{7,5},{... | collective-permute-start | bytes 589832 | tf_op jit(solution)/shard_map/ppermute | solution.py:24
  311.5 13.7 %collective-permute-start.4 = (bf16[128,768]{0,1:T(8,128)(2,1)S(1)}, bf16[128,768]{0,1:T(8,128)(2,1)S(1)}, u32[]{:S(2)}, u32[]{:S(2)}) collective-permute-start(bf16[128,768]{0,1:T(8,128)(2,1)S(1)} %get-tuple-element.6), channel_id=1, source_target_pairs={{0,2},{2,4},{4,6},{6,8},{8,10},{10,12},{12,14},{1,3},{3,5},{5,7},{... | collective-permute-start | bytes 589832 | tf_op jit(solution)/shard_map/ppermute | solution.py:22
  315.9 9.4 %collective-permute-start.5 = (bf16[128,768]{0,1:T(8,128)(2,1)S(1)}, bf16[128,768]{0,1:T(8,128)(2,1)S(1)}, u32[]{:S(2)}, u32[]{:S(2)}) collective-permute-start(bf16[128,768]{0,1:T(8,128)(2,1)S(1)} %get-tuple-element.7), channel_id=1, source_target_pairs={{2,0},{4,2},{6,4},{8,6},{10,8},{12,10},{14,12},{3,1},{5,3},{7,5},{... | collective-permute-start | bytes 589832 | tf_op jit(solution)/shard_map/ppermute | solution.py:24
  (60 other events, 136.6 us)
Sparse Core Ops, SparseCore 0:
  10.2 40.0 all-gather.10
  52.5 64.2 all-gather.4
  119.0 46.7 all-gather.6
  167.8 64.2 all-gather.8
where the time goes:
time: 340 us; the launch traced here: 334 us
  waiting for transfers between devices  201 us (59%)
  matrix products  48.9 us (14%)
  starting transfers between devices  38.5 us (11%)
  local copies, waits for them, and re-layouts  19.3 us (6%)
  between operations  15.9 us (5%)
  other arithmetic  10.7 us (3%)
    all_gather x1, waiting for transfers between devices, local(): lax.all_gather(w_qkv_time, 'space', axis=0, tiled=True)  60.6 us
    all_gather x1, waiting for transfers between devices, local(): lax.all_gather(w_qkv_space, 'space', axis=0, tiled=True)  51.4 us
    all_gather x1, waiting for transfers between devices, local(): lax.all_gather(w_out_time, 'space', axis=0, tiled=True)  39.2 us
    all_gather x1, waiting for transfers between devices, local(): lax.all_gather(w_out_space, 'space', axis=0, tiled=True)  18 us
    ppermute x4, waiting for transfers between devices, padded(): lax.ppermute(tail, axis, [(i, (i + 1) % count) for i in range(ends)])  17.2 us
    ppermute x4, starting transfers between devices, padded(): lax.ppermute(tail, axis, [(i, (i + 1) % count) for i in range(ends)])  15.2 us
    dot_general x6, matrix products, space_back(): jnp.einsum('gst,sgh->tgh', probability, grad_part, preferred_element_type...  8.4 us
    all_to_all x2, waiting for transfers between devices, to_frames(): lax.all_to_all(local_rows[None], 'frame', split_axis=1, concat_axis=0, ti...  8.21 us
  transfers between devices with their start and end apart: 16, of which 10 were waited for; matrix products, arithmetic and copies ran while one was open for 9% of the time, Pallas kernels for 0%

commit v1 on v0

v1 whole, which is shorter than its diff:
```python
import functools

import jax
import jax.numpy as jnp
from jax import lax
from jax.experimental import pallas as pl
from jax.experimental.pallas import tpu as pltpu
from jax.sharding import PartitionSpec as P

HEADS = 12
HD = 64
D = 768
ROWS = 128
PAIRS = HEADS // 2
EPS = 1e-06
FAR = -1e30
SCALE = HD ** (-0.5)
F32 = jnp.float32
BF16 = jnp.bfloat16
TILE = 256


def dot(a, b):
    return jnp.dot(a, b, preferred_element_type=F32)


def dot_nt(a, b):
    return lax.dot_general(a, b, (((1,), (1,)), ((), ())), preferred_element_type=F32)


def dot_tn(a, b):
    return lax.dot_general(a, b, (((0,), (0,)), ((), ())), preferred_element_type=F32)


def rms_factor(values):
    return lax.rsqrt(jnp.mean(values * values, axis=-1, keepdims=True) + EPS)


def rms_back(values, upstream):
    factor = rms_factor(values)
    inner = jnp.mean(values * upstream, axis=-1, keepdims=True)
    return factor * upstream - values * (factor * factor * factor * inner)


def remote(src, dst, send, recv, where):
    return pltpu.make_async_remote_copy(
        src_ref=src,
        dst_ref=dst,
        send_sem=send,
        recv_sem=recv,
        device_id=where,
        device_id_type=pl.DeviceIdType.MESH,
    )


class Gather:
    X = 2
    Z = 4

    def __init__(self, weights, sems):
        self.w = weights
        self.zs, self.zr, self.xs, self.xr, self.ys, self.yr, self.cs, self.cr = sems
        self.s = lax.axis_index("space")
        self.z = self.s // self.X
        self.x = self.s % self.X
        self.odd = lax.axis_index("frame")
        self.c = lax.axis_index("dp")

    def rows(self, group, shard, offset, count):
        start = pl.multiple_of(shard * 96 + offset, 16)
        return self.w.at[group, pl.ds(start, count), :]

    def main(self, group, shard):
        return self.rows(group, shard, 48 * self.c + 16 * self.odd, 32)

    def along_z(self, group, step, at):
        ref = self.main(group, at * self.X + self.x)
        way = 0 if step > 0 else 1
        return remote(
            ref, ref, self.zs.at[group, way, at], self.zr.at[group, at], {"space": self.s + step * self.X}
        )

    def along_x(self, group, at, column):
        ref = self.main(group, at * self.X + column)
        partner = self.s + 1 - 2 * self.x
        return remote(ref, ref, self.xs.at[group, at], self.xr.at[group, at], {"space": partner})

    def along_y(self, group, shard, sending):
        which = self.odd if sending else 1 - self.odd
        ref = self.rows(group, shard, 48 * self.c + 32 * which, 16)
        return remote(
            ref, ref, self.ys.at[group, shard], self.yr.at[group, shard], {"frame": 1 - self.odd}
        )

    def across(self, group, shard, sending):
        half = self.c if sending else 1 - self.c
        ref = self.rows(group, shard, 48 * half, 48)
        return remote(
            ref, ref, self.cs.at[group, shard], self.cr.at[group, shard], {"dp": 1 - self.c}
        )

    def open(self, group):
        @pl.when(self.z < self.Z - 1)
        def _():
            self.along_z(group, 1, self.z).start()

        @pl.when(self.z > 0)
        def _():
            self.along_z(group, -1, self.z).start()

        self.along_x(group, self.z, self.x).start()

    def z_step(self, group, distance):
        for step in (1, -1):
            at = self.z - step * distance

            @pl.when((at >= 0) & (at < self.Z))
            def _():
                self.along_z(group, -step, at).wait_recv()
                onward = (self.z + step >= 0) & (self.z + step < self.Z)

                @pl.when(onward)
                def _():
                    self.along_z(group, step, at).start()

                self.along_x(group, at, self.x).start()
                self.along_y(group, at * self.X + self.x, True).start()

    def x_step(self, group, distance):
        for step in (1, -1) if distance else (1,):
            at = self.z - step * distance

            @pl.when((at >= 0) & (at < self.Z))
            def _():
                self.along_x(group, at, 1 - self.x).wait_recv()
                self.along_y(group, at * self.X + 1 - self.x, True).start()

    def zx_stage(self, group):
        for distance in range(1, self.Z):
            self.z_step(group, distance)
            self.x_step(group, distance - 1)
        self.x_step(group, self.Z - 1)

    def others(self):
        count = self.X * self.Z
        return [lax.rem(self.s + k, count) for k in range(1, count)]

    def y_stage(self, group):
        for shard in self.others():
            self.along_y(group, shard, False).wait_recv()
            self.across(group, shard, True).start()

    def c_stage(self, group):
        for shard in self.others():
            self.across(group, shard, False).wait_recv()

    def close(self, group):
        for at in range(self.Z):

            @pl.when((self.z < self.Z - 1) & (at <= self.z))
            def _():
                self.along_z(group, 1, at).wait_send()

            @pl.when((self.z > 0) & (at >= self.z))
            def _():
                self.along_z(group, -1, at).wait_send()

            self.along_x(group, at, self.x).wait_send()
        for shard in self.others():
            self.along_y(group, shard, True).wait_send()
            self.across(group, shard, True).wait_send()


def kernel(
    frames, count, gathers,
    x_ref, cot_ref, wqs_ref, wos_ref, wqt_ref, wot_ref, nb_ref,
    out_ref, grad_ref,
    weights, q_buf, kv_win, att, probs, stream, rows_a, big, tsend, tgot, usend, ugot,
    attn_t, grads, gown, gsend, ggot, acc,
    load_sem, zs, zr, xs, xr, ys, yr, cs, cr, hs, hr, bs, br, ts, tr, us, ur,
):
    s = lax.axis_index("space")
    f = lax.axis_index("frame")
    c = lax.axis_index("dp")

    barrier = pltpu.get_barrier_semaphore()
    peers = [{"space": lax.rem(s + k, count)} for k in (1, 2, count - 2, count - 1)]
    peers += [{"frame": lax.rem(f + k, frames)} for k in range(1, frames)]
    peers += [{"dp": 1 - c}]
    for peer in peers:
        pl.semaphore_signal(barrier, inc=1, device_id=peer, device_id_type=pl.DeviceIdType.MESH)

    depth = wqs_ref.shape[0]
    start = pl.multiple_of(s * depth, 16) if gathers else 0
    here = pl.ds(start, depth)
    loads = [
        pltpu.make_async_copy(ref, weights.at[group, here, pl.ds(col, ref.shape[1])], load_sem.at[i])
        for i, (ref, group, col) in enumerate(
            ((wqs_ref, 0, 0), (wos_ref, 0, 3 * D), (wqt_ref, 1, 0), (wot_ref, 1, 3 * D))
        )
    ]
    for load in loads:
        load.start()

    lane = lax.broadcasted_iota(jnp.int32, (1, 2 * HD), 1)
    first = lane < HD
    first_row = first.astype(F32).astype(BF16)
    second_row = (1.0 - first.astype(F32)).astype(BF16)

    def stacked(pair):
        return jnp.concatenate([pair * first_row, pair * second_row], axis=0)

    def joined(both):
        return jnp.where(first, both[:ROWS], both[ROWS:])

    def forward(rows, group, col, width, put):
        def body(i, carry):
            at = pl.multiple_of(i * TILE, TILE)
            put(at, dot(rows[...], weights[group, :, pl.ds(col + at, TILE)]))
            return carry

        lax.fori_loop(0, width // TILE, body, 0)

    def backward(rows, cols, group, put):
        def body(i, carry):
            at = pl.multiple_of(i * TILE, TILE)
            put(at, dot_nt(rows[...], weights[group, pl.ds(at, TILE), cols]))
            return carry

        lax.fori_loop(0, D // TILE, body, 0)

    def into(ref, col=0):
        def put(at, value):
            ref[:, pl.ds(col + at, TILE)] = value.astype(ref.dtype)

        return put

    values = x_ref[...].astype(F32)
    rows_a[...] = (values * rms_factor(values)).astype(BF16)

    @pl.when(s == 0)
    def _():
        kv_win[0:ROWS, :] = jnp.zeros((ROWS, 2 * D), BF16)
        ggot[0] = jnp.zeros((ROWS, 2 * D), BF16)

    @pl.when(s == count - 1)
    def _():
        kv_win[2 * ROWS : 3 * ROWS, :] = jnp.zeros((ROWS, 2 * D), BF16)
        ggot[1] = jnp.zeros((ROWS, 2 * D), BF16)

    for load in loads:
        load.wait()
    pl.semaphore_wait(barrier, len(peers))

    gather = Gather(weights, (zs, zr, xs, xr, ys, yr, cs, cr)) if gathers else None
    if gathers:
        gather.open(0)
        gather.open(1)
        gather.zx_stage(0)
        gather.y_stage(0)
        gather.c_stage(0)

    def put_kv(at, value):
        kv_win[ROWS : 2 * ROWS, pl.ds(at, TILE)] = value.astype(BF16)

    forward(rows_a, 0, D, 2 * D, put_kv)
    mine = kv_win.at[pl.ds(ROWS, ROWS), :]
    halo = [
        remote(mine, kv_win.at[pl.ds(2 * ROWS, ROWS), :], hs.at[0], hr.at[0], {"space": s - 1}),
        remote(mine, kv_win.at[pl.ds(0, ROWS), :], hs.at[1], hr.at[1], {"space": s + 1}),
    ]
    back_halo = [
        remote(gsend.at[0], ggot.at[1], bs.at[0], br.at[0], {"space": s - 1}),
        remote(gsend.at[1], ggot.at[0], bs.at[1], br.at[1], {"space": s + 1}),
    ]
    has = [s > 0, s < count - 1]

    def each_way(action):
        for way in range(2):
            pl.when(has[way])(functools.partial(action, way))

    each_way(lambda way: halo[way].start())
    forward(rows_a, 0, 0, D, into(q_buf))

    if gathers:
        gather.zx_stage(1)

    each_way(lambda way: halo[1 - way].wait_recv())

    def listed(block):
        hit = nb_ref[s, 0] == block
        for j in range(1, nb_ref.shape[1]):
            hit = hit | (nb_ref[s, j] == block)
        return jnp.where(hit, 0.0, FAR).astype(F32)

    key_lane = lax.broadcasted_iota(jnp.int32, (1, 3 * ROWS), 1)
    bias = jnp.where(
        key_lane < ROWS, listed(s - 1), jnp.where(key_lane < 2 * ROWS, listed(s), listed(s + 1))
    )

    def attend(hp, carry):
        cols = pl.ds(pl.multiple_of(hp * 128, 128), 128)
        vcols = pl.ds(pl.multiple_of(D + hp * 128, 128), 128)
        scores = dot_nt(stacked(q_buf[:, cols]), kv_win[:, cols]) * SCALE + bias
        expo = jnp.exp(scores)
        weight = expo / jnp.sum(expo, axis=-1, keepdims=True)
        probs[hp] = weight
        att[:, cols] = joined(dot(weight.astype(BF16), kv_win[:, vcols])).astype(BF16)
        return carry

    lax.fori_loop(0, PAIRS, attend, 0)

    if gathers:
        gather.y_stage(1)

    forward(att, 0, 3 * D, D, into(acc))
    stream[...] = (x_ref[...].astype(F32) + acc[...]).astype(BF16)
    values = stream[...].astype(F32)
    rows_a[...] = (values * rms_factor(values)).astype(BF16)

    if gathers:
        gather.c_stage(1)

    forward(rows_a, 1, D, 2 * D, into(tsend.at[0]))
    forward(rows_a, 1, 0, D, into(tsend.at[1]))
    backward(cot_ref, pl.ds(3 * D, D), 1, into(tsend.at[1], D))

    def to_frame(k):
        return remote(
            tsend.at[(f + k) // frames], tgot.at[f], ts.at[k - 1], tr.at[f], {"frame": lax.rem(f + k, frames)}
        )

    def from_frame(k):
        o = lax.rem(f + k, frames)
        return remote(tsend.at[0], tgot.at[o], ts.at[k - 1], tr.at[o], {"frame": o})

    def pairs_to(k):
        return remote(
            usend.at[k - 1], ugot.at[f], us.at[k - 1], ur.at[f], {"frame": lax.rem(f + k, frames)}
        )

    def pairs_from(k):
        o = lax.rem(f + k, frames)
        return remote(usend.at[k - 1], ugot.at[o], us.at[k - 1], ur.at[o], {"frame": o})

    for k in range(1, frames):
        to_frame(k).start()

    hot = (
        lax.broadcasted_iota(jnp.int32, (D, 128), 0) // HD
        == lax.broadcasted_iota(jnp.int32, (D, 128), 1)
    ).astype(F32).astype(BF16)

    def per_head(product):
        high = product.astype(BF16)
        low = (product - high.astype(F32)).astype(BF16)
        return dot(high, hot) + dot(low, hot)

    def spread(heads):
        return dot_nt(heads, hot)

    query = tsend[1, :, 0:D].astype(F32)
    grad_att = tsend[1, :, D : 2 * D].astype(F32)

    def pair_terms(held):
        key = held[:, 0:D].astype(F32)
        value = held[:, D : 2 * D].astype(F32)
        return per_head(query * key) * SCALE, per_head(grad_att * value)

    score, prob_grad = pair_terms(tsend[0])
    expos = [jnp.exp(score)]
    prob_grads = [prob_grad]
    for k in range(1, frames):
        from_frame(k).wait_recv()
        o = lax.rem(f + k, frames)
        score, prob_grad = pair_terms(tgot[o])
        expos.append(jnp.exp(score + jnp.where(o < f, 0.0, FAR).astype(F32)))
        prob_grads.append(prob_grad)
    total = sum(expos[1:], expos[0])
    shares = [expo / total for expo in expos]
    rounded = [share.astype(BF16) for share in shares]

    def held_at(k):
        return tsend[0] if k == 0 else tgot[lax.rem(f + k, frames)]

    update = spread(rounded[0]) * held_at(0)[:, D : 2 * D].astype(F32)
    for k in range(1, frames):
        update = update + spread(rounded[k]) * held_at(k)[:, D : 2 * D].astype(F32)
    attn_t[...] = update.astype(BF16)
    delta = per_head(grad_att * attn_t[...].astype(F32))
    score_grads = [
        (share * (grad - delta)).astype(BF16) for share, grad in zip(shares, prob_grads)
    ]
    for k in range(1, frames):
        usend[k - 1, :, 0:128] = rounded[k]
        usend[k - 1, :, 128:256] = score_grads[k]
        pairs_to(k).start()

    def put_out(at, value):
        cols = pl.ds(at, TILE)
        out_ref[:, cols] = (stream[:, cols].astype(F32) + value).astype(BF16)

    forward(attn_t, 1, 3 * D, D, put_out)

    update = spread(score_grads[0]) * held_at(0)[:, 0:D].astype(F32)
    for k in range(1, frames):
        update = update + spread(score_grads[k]) * held_at(k)[:, 0:D].astype(F32)
    grads[:, 0:D] = (update * SCALE).astype(BF16)

    key_grad = spread(score_grads[0]) * query
    value_grad = spread(rounded[0]) * grad_att
    for k in range(1, frames):
        pairs_from(k).wait_recv()
        o = lax.rem(f + k, frames)
        key_grad = key_grad + spread(ugot[o, :, 128:256]) * tgot[o, :, 0:D].astype(F32)
        value_grad = value_grad + spread(ugot[o, :, 0:128]) * tgot[o, :, D : 2 * D].astype(F32)
    grads[:, D : 2 * D] = (key_grad * SCALE).astype(BF16)
    grads[:, 2 * D : 3 * D] = value_grad.astype(BF16)

    backward(grads, pl.ds(0, 3 * D), 1, into(acc))
    rows_a[...] = (
        cot_ref[...].astype(F32) + rms_back(stream[...].astype(F32), acc[...])
    ).astype(BF16)

    backward(rows_a, pl.ds(3 * D, D), 0, into(big))

    def attend_back(hp, carry):
        cols = pl.ds(pl.multiple_of(hp * 128, 128), 128)
        vcols = pl.ds(pl.multiple_of(D + hp * 128, 128), 128)
        key = kv_win[:, cols]
        grad_two = stacked(big[:, cols])
        query_two = stacked(q_buf[:, cols])
        weight = probs[hp]
        grad_prob = dot_nt(grad_two, kv_win[:, vcols])
        held = att[:, cols].astype(F32)
        row_delta = jnp.sum(
            grad_two.astype(F32) * jnp.concatenate([held, held], axis=0), axis=-1, keepdims=True
        )
        score_grad = (weight * (grad_prob - row_delta)).astype(BF16)
        grads[:, cols] = (joined(dot(score_grad, key)) * SCALE).astype(BF16)
        key_part = dot_tn(score_grad, query_two) * SCALE
        value_part = dot_tn(weight.astype(BF16), grad_two)
        for part, at in ((key_part, cols), (value_part, vcols)):
            gsend[0, :, at] = part[:ROWS].astype(BF16)
            gown[:, at] = part[ROWS : 2 * ROWS]
            gsend[1, :, at] = part[2 * ROWS :].astype(BF16)
        return carry

    lax.fori_loop(0, PAIRS, attend_back, 0)
    each_way(lambda way: back_halo[way].start())
    backward(grads.at[:, pl.ds(0, D)], pl.ds(0, D), 0, into(acc))
    each_way(lambda way: back_halo[1 - way].wait_recv())
    grads[:, D : 3 * D] = (
        gown[...] + ggot[0].astype(F32) + ggot[1].astype(F32)
    ).astype(BF16)

    def put_more(at, value):
        cols = pl.ds(at, TILE)
        acc[:, cols] = acc[:, cols] + value

    backward(grads.at[:, pl.ds(D, 2 * D)], pl.ds(D, 2 * D), 0, put_more)
    grad_ref[...] = (
        rows_a[...].astype(F32) + rms_back(x_ref[...].astype(F32), acc[...])
    ).astype(BF16)

    each_way(lambda way: halo[way].wait_send())
    each_way(lambda way: back_halo[way].wait_send())
    for k in range(1, frames):
        to_frame(k).wait_send()
        pairs_to(k).wait_send()
    if gathers:
        gather.close(0)
        gather.close(1)


def local(frames, count, frames_in, cotangent, w_qkv_space, w_out_space, w_qkv_time, w_out_time, neighbours):
    gathers = frames == 2 and count == 8 and w_qkv_space.shape[0] == 96
    blocks = [w_qkv_space, w_out_space, w_qkv_time, w_out_time]
    if not gathers:
        blocks = [lax.all_gather(block, "space", axis=0, tiled=True) for block in blocks]
    vmem = pl.BlockSpec(memory_space=pltpu.VMEM)
    hbm = pl.BlockSpec(memory_space=pl.ANY)
    dma = pltpu.SemaphoreType.DMA
    wide = (ROWS, 2 * D)
    out, grad = pl.pallas_call(
        functools.partial(kernel, frames, count, gathers),
        out_shape=[jax.ShapeDtypeStruct((ROWS, D), BF16)] * 2,
        in_specs=[vmem, vmem, hbm, hbm, hbm, hbm, pl.BlockSpec(memory_space=pltpu.SMEM)],
        out_specs=[vmem, vmem],
        scratch_shapes=[
            pltpu.VMEM((2, D, 4 * D), BF16),
            pltpu.VMEM((ROWS, D), BF16),
            pltpu.VMEM((3 * ROWS, 2 * D), BF16),
            pltpu.VMEM((ROWS, D), BF16),
            pltpu.VMEM((PAIRS, 2 * ROWS, 3 * ROWS), F32),
            pltpu.VMEM((ROWS, D), BF16),
            pltpu.VMEM((ROWS, D), BF16),
            pltpu.VMEM((ROWS, D), BF16),
            pltpu.VMEM((2,) + wide, BF16),
            pltpu.VMEM((frames,) + wide, BF16),
            pltpu.VMEM((frames - 1, ROWS, 256), BF16),
            pltpu.VMEM((frames, ROWS, 256), BF16),
            pltpu.VMEM((ROWS, D), BF16),
            pltpu.VMEM((ROWS, 3 * D), BF16),
            pltpu.VMEM(wide, F32),
            pltpu.VMEM((2,) + wide, BF16),
            pltpu.VMEM((2,) + wide, BF16),
            pltpu.VMEM((ROWS, D), F32),
            dma((4,)),
            dma((2, 2, 4)), dma((2, 4)), dma((2, 4)), dma((2, 4)),
            dma((2, 8)), dma((2, 8)), dma((2, 8)), dma((2, 8)),
            dma((2,)), dma((2,)), dma((2,)), dma((2,)),
            dma((frames - 1,)), dma((frames,)), dma((frames - 1,)), dma((frames,)),
        ],
        compiler_params=pltpu.CompilerParams(
            collective_id=0, has_side_effects=True, vmem_limit_bytes=56 * 1024 * 1024
        ),
    )(frames_in[0], cotangent[0], *blocks, neighbours)
    return out[None], grad[None]


def solution(mesh):
    rows = P(("dp", "frame"), "space", None)
    held = P("space", None)
    return jax.shard_map(
        functools.partial(local, mesh.shape["frame"], mesh.shape["space"]),
        mesh=mesh,
        in_specs=(rows, rows, held, held, held, held, P()),
        out_specs=(rows, rows),
        check_vma=False,
    )
```

time: 340 us -> 118 us (0.35); the launches traced: 334 us -> 118 us
  waiting for transfers between devices: 201 us -> 0 us
  Pallas kernels: 0 us -> 113 us
  matrix products: 48.9 us -> 0 us
  starting transfers between devices: 38.5 us -> 0 us
  local copies, waits for them, and re-layouts: 19.3 us -> 3.68 us
  between operations: 15.9 us -> 0.66 us
  other arithmetic: 10.7 us -> 0 us
    all_gather x4 -> x0, waiting for transfers between devices: 169 us -> none  [the longest x1 60.6 us: local(): lax.all_gather(w_qkv_time, 'space', axis=0, tiled=True)]
    pallas_call x0 -> x1, Pallas kernels: none -> 113 us  [local(): pl.pallas_call(functools.partial(kernel, frames, count, gathers), out_sha...]
    dot_general x50 -> x0, matrix products: 41.1 us -> none  [the longest x6 8.4 us: space_back(): jnp.einsum('gst,sgh->tgh', probability, grad_part, preferred_element_type...]
    ppermute x8 -> x0, starting transfers between devices: 23.2 us -> none  [the longest x4 15.2 us: padded(): lax.ppermute(tail, axis, [(i, (i + 1) % count) for i in range(ends)])]
    ppermute x8 -> x0, waiting for transfers between devices: 17.2 us -> none  [the longest x4 17.2 us: padded(): lax.ppermute(tail, axis, [(i, (i + 1) % count) for i in range(ends)])]
    all_to_all x4 -> x0, starting transfers between devices: 15.1 us -> none  [the longest x2 7.93 us: to_space(): lax.all_to_all(frame_rows, 'frame', split_axis=0, concat_axis=1, tiled=True)]
    all_to_all x4 -> x0, waiting for transfers between devices: 12 us -> none  [the longest x2 8.21 us: to_frames(): lax.all_to_all(local_rows[None], 'frame', split_axis=1, concat_axis=0, ti...]
    div x6 -> x0, matrix products: 7.79 us -> none  [space_attend(): probability = (exponent / totals[:, :, None]).astype(jnp.bfloat16)]
  transfers between devices with their start and end apart: 16 -> 0, of which waited for: 10 -> 0; matrix products, arithmetic and copies ran while one was open for 9% -> 0% of each run, Pallas kernels for 0% -> 0%
where the time goes in v1:
time: 118 us
  Pallas kernels  113 us (96%)
  local copies, waits for them, and re-layouts  3.68 us (3%)
    pallas_call x1, Pallas kernels, local(): pl.pallas_call(functools.partial(kernel, frames, count, gathers), out_sha...  113 us
    unnamed x7, local copies, waits for them, and re-layouts  3.68 us

profile of v1, /device:TPU:3, one launch (start us, length us, event | category | flops | bytes accessed | tf_op | source)
XLA Modules:
  0.0 117.6 jit_solution(15478298412337771432)
XLA Ops:
  0.6 0.0 copy-start.1
  0.6 0.7 copy-done.1
  1.3 0.7 copy.9.nb_ref
  2.0 113.3 %shard_map.86 = (bf16[128,768]{1,0:T(8,128)(2,1)}, bf16[128,768]{1,0:T(8,128)(2,1)}) custom-call(bf16[128,768]{1,0:T(8,128)(2,1)} %bitcast.4, bf16[128,768]{1,0:T(8,128)(2,1)} %bitcast.5, bf16[96,2304]{1,0:T(8,128)(2,1)} %wqs_ref.1, bf16[96,768]{1,0:T(8,128)(2,1)} %wos_ref.1, bf16[96,2304]{1,0:T(8,128)(2,1)} %wqt_ref.1, bf16[96,768]{1,0:T(8,128)(2,1)} %wot_ref.1, ...), custom_call_target="tpu_custom_call" | custom-call | tf_op jit(solution)/shard_map/pallas_call | solution.py:485
  115.3 0.0 copy-start
  115.3 1.7 %copy.12 = bf16[1,128,768]{2,1,0:T(8,128)(2,1)} copy(bf16[1,128,768]{2,1,0:T(8,128)(2,1)} %bitcast.7) | data formatting | bytes 393216
  116.9 0.0 copy-done
  116.9 0.7 copy.13
Async XLA Ops:
  0.6 0.7 copy-start.1
  115.3 1.7 %copy-start = (bf16[128,768]{1,0:T(8,128)(2,1)S(1)}, bf16[128,768]{1,0:T(8,128)(2,1)}, u32[]{:S(2)}) copy-start(bf16[128,768]{1,0:T(8,128)(2,1)} %get-tuple-element.5) | copy-start | bytes 589828

commit v2 on v1

--- a/solution.py
+++ b/solution.py
@@ -135,12 +135,6 @@
                 self.along_x(group, at, 1 - self.x).wait_recv()
                 self.along_y(group, at * self.X + 1 - self.x, True).start()
 
-    def zx_stage(self, group):
-        for distance in range(1, self.Z):
-            self.z_step(group, distance)
-            self.x_step(group, distance - 1)
-        self.x_step(group, self.Z - 1)
-
     def others(self):
         count = self.X * self.Z
         return [lax.rem(self.s + k, count) for k in range(1, count)]
@@ -175,9 +169,9 @@
     frames, count, gathers,
     x_ref, cot_ref, wqs_ref, wos_ref, wqt_ref, wot_ref, nb_ref,
     out_ref, grad_ref,
-    weights, q_buf, kv_win, att, probs, stream, rows_a, big, tsend, tgot, usend, ugot,
-    attn_t, grads, gown, gsend, ggot, acc,
-    load_sem, zs, zr, xs, xr, ys, yr, cs, cr, hs, hr, bs, br, ts, tr, us, ur,
+    weights, x_win, normed, qkv, att, probs, near_probs, stream, rows_a, tsend, tgot, usend, ugot,
+    attn_t, grads, gown, ga_win, tot, tot_got, dlt, dlt_got, acc,
+    load_sem, zs, zr, xs, xr, ys, yr, cs, cr, hs, hr, bs, br, ds, dr, es, er, ts, tr, us, ur,
 ):
     s = lax.axis_index("space")
     f = lax.axis_index("frame")
@@ -235,57 +229,66 @@
 
         return put
 
-    values = x_ref[...].astype(F32)
-    rows_a[...] = (values * rms_factor(values)).astype(BF16)
-
-    @pl.when(s == 0)
-    def _():
-        kv_win[0:ROWS, :] = jnp.zeros((ROWS, 2 * D), BF16)
-        ggot[0] = jnp.zeros((ROWS, 2 * D), BF16)
-
-    @pl.when(s == count - 1)
-    def _():
-        kv_win[2 * ROWS : 3 * ROWS, :] = jnp.zeros((ROWS, 2 * D), BF16)
-        ggot[1] = jnp.zeros((ROWS, 2 * D), BF16)
+    own = pl.ds(ROWS, ROWS)
+    sides = (pl.ds(0, ROWS), pl.ds(2 * ROWS, ROWS))
+    has = [s > 0, s < count - 1]
+
+    def two_ways(src, slots, send, recv):
+        return [
+            remote(src, slots[1 - way], send.at[way], recv.at[way], {"space": s + 2 * way - 1})
+            for way in range(2)
+        ]
+
+    def each_way(action):
+        for way in range(2):
+            pl.when(has[way])(functools.partial(action, way))
+
+    def leave(copies):
+        each_way(lambda way: copies[way].start())
+
+    def arrive(copies):
+        each_way(lambda way: copies[1 - way].wait_recv())
+
+    x_halo = two_ways(x_ref, [x_win.at[side, :] for side in sides], hs, hr)
+    ga_halo = two_ways(ga_win.at[own, :], [ga_win.at[side, :] for side in sides], bs, br)
+    tot_halo = two_ways(tot, [tot_got.at[way] for way in range(2)], ds, dr)
+    dlt_halo = two_ways(dlt, [dlt_got.at[way] for way in range(2)], es, er)
+
+    x_win[own, :] = x_ref[...]
+    for way in range(2):
+
+        @pl.when(jnp.logical_not(has[way]))
+        def _():
+            x_win[sides[way], :] = jnp.zeros((ROWS, D), BF16)
+            ga_win[sides[way], :] = jnp.zeros((ROWS, D), BF16)
+            tot_got[way] = jnp.ones((ROWS, 128), F32)
+            dlt_got[way] = jnp.zeros((ROWS, 128), F32)
 
     for load in loads:
         load.wait()
     pl.semaphore_wait(barrier, len(peers))
 
+    leave(x_halo)
     gather = Gather(weights, (zs, zr, xs, xr, ys, yr, cs, cr)) if gathers else None
-    if gathers:
-        gather.open(0)
-        gather.open(1)
-        gather.zx_stage(0)
-        gather.y_stage(0)
-        gather.c_stage(0)
-
-    def put_kv(at, value):
-        kv_win[ROWS : 2 * ROWS, pl.ds(at, TILE)] = value.astype(BF16)
-
-    forward(rows_a, 0, D, 2 * D, put_kv)
-    mine = kv_win.at[pl.ds(ROWS, ROWS), :]
-    halo = [
-        remote(mine, kv_win.at[pl.ds(2 * ROWS, ROWS), :], hs.at[0], hr.at[0], {"space": s - 1}),
-        remote(mine, kv_win.at[pl.ds(0, ROWS), :], hs.at[1], hr.at[1], {"space": s + 1}),
-    ]
-    back_halo = [
-        remote(gsend.at[0], ggot.at[1], bs.at[0], br.at[0], {"space": s - 1}),
-        remote(gsend.at[1], ggot.at[0], bs.at[1], br.at[1], {"space": s + 1}),
-    ]
-    has = [s > 0, s < count - 1]
-
-    def each_way(action):
-        for way in range(2):
-            pl.when(has[way])(functools.partial(action, way))
-
-    each_way(lambda way: halo[way].start())
-    forward(rows_a, 0, 0, D, into(q_buf))
-
-    if gathers:
-        gather.zx_stage(1)
-
-    each_way(lambda way: halo[1 - way].wait_recv())
+
+    def pass_on(*steps):
+        if gathers:
+            for name, *where in steps:
+                getattr(gather, name)(*where)
+
+    pass_on(
+        ("open", 0), ("open", 1),
+        ("z_step", 0, 1), ("x_step", 0, 0), ("z_step", 0, 2), ("x_step", 0, 1), ("z_step", 0, 3),
+        ("x_step", 0, 2), ("z_step", 1, 1), ("x_step", 0, 3),
+    )
+    arrive(x_halo)
+    values = x_win[...].astype(F32)
+    normed[...] = (values * rms_factor(values)).astype(BF16)
+    pass_on(("y_stage", 0), ("z_step", 1, 2), ("x_step", 1, 0), ("c_stage", 0))
+    forward(normed, 0, 0, D, into(qkv))
+    pass_on(("z_step", 1, 3), ("x_step", 1, 1))
+    forward(normed, 0, D, 2 * D, into(qkv, D))
+    pass_on(("x_step", 1, 2), ("x_step", 1, 3))
 
     def listed(block):
         hit = nb_ref[s, 0] == block
@@ -298,17 +301,24 @@
         key_lane < ROWS, listed(s - 1), jnp.where(key_lane < 2 * ROWS, listed(s), listed(s + 1))
     )
 
-    def attend(hp, carry):
-        cols = pl.ds(pl.multiple_of(hp * 128, 128), 128)
-        vcols = pl.ds(pl.multiple_of(D + hp * 128, 128), 128)
-        scores = dot_nt(stacked(q_buf[:, cols]), kv_win[:, cols]) * SCALE + bias
+    head_lane = lax.broadcasted_iota(jnp.int32, (1, 128), 1)
+
+    def cols_of(hp, part):
+        return pl.ds(pl.multiple_of(part * D + hp * 128, 128), 128)
+
+    def attend(hp, totals):
+        cols = cols_of(hp, 0)
+        scores = dot_nt(stacked(qkv[own, cols]), qkv[:, cols_of(hp, 1)]) * SCALE + bias
         expo = jnp.exp(scores)
-        weight = expo / jnp.sum(expo, axis=-1, keepdims=True)
+        total = jnp.sum(expo, axis=-1, keepdims=True)
+        weight = expo / total
         probs[hp] = weight
-        att[:, cols] = joined(dot(weight.astype(BF16), kv_win[:, vcols])).astype(BF16)
-        return carry
-
-    lax.fori_loop(0, PAIRS, attend, 0)
+        att[:, cols] = joined(dot(weight.astype(BF16), qkv[:, cols_of(hp, 2)])).astype(BF16)
+        totals = jnp.where(head_lane == 2 * hp, total[:ROWS], totals)
+        return jnp.where(head_lane == 2 * hp + 1, total[ROWS:], totals)
+
+    tot[...] = lax.fori_loop(0, PAIRS, attend, jnp.ones((ROWS, 128), F32))
+    leave(tot_halo)
 
     if gathers:
         gather.y_stage(1)
@@ -321,18 +331,65 @@
     if gathers:
         gather.c_stage(1)
 
-    forward(rows_a, 1, D, 2 * D, into(tsend.at[0]))
+    def frame_copy(k, half, o, slot):
+        cols = pl.ds(half * D, D)
+        return remote(
+            tsend.at[(f + k) // frames, :, cols], tgot.at[slot, :, cols],
+            ts.at[k - 1, half], tr.at[slot, half], {"frame": o},
+        )
+
+    def to_frame(k, half):
+        return frame_copy(k, half, lax.rem(f + k, frames), f)
+
+    def from_frame(k, half):
+        o = lax.rem(f + k, frames)
+        return frame_copy(k, half, o, o)
+
+    def to_later(half):
+        for k in range(1, frames):
+            pl.when(f + k < frames)(lambda: to_frame(k, half).start())
+
+    def to_earlier(half):
+        for k in range(1, frames):
+            pl.when(f + k >= frames)(lambda: to_frame(k, half).start())
+
+    forward(rows_a, 1, D, D, into(tsend.at[0]))
+    to_later(0)
+    forward(rows_a, 1, 2 * D, D, into(tsend.at[0], D))
+    to_later(1)
     forward(rows_a, 1, 0, D, into(tsend.at[1]))
+    to_earlier(0)
     backward(cot_ref, pl.ds(3 * D, D), 1, into(tsend.at[1], D))
-
-    def to_frame(k):
-        return remote(
-            tsend.at[(f + k) // frames], tgot.at[f], ts.at[k - 1], tr.at[f], {"frame": lax.rem(f + k, frames)}
-        )
-
-    def from_frame(k):
-        o = lax.rem(f + k, frames)
-        return remote(tsend.at[0], tgot.at[o], ts.at[k - 1], tr.at[o], {"frame": o})
+    to_earlier(1)
+
+    def listed_by(block):
+        row = jnp.clip(block, 0, count - 1)
+        hit = nb_ref[row, 0] == s
+        for j in range(1, nb_ref.shape[1]):
+            hit = hit | (nb_ref[row, j] == s)
+        return jnp.where(hit & (block >= 0) & (block < count), 0.0, FAR).astype(F32)
+
+    def both_sides(window, cols):
+        return jnp.concatenate([stacked(window[side, cols]) for side in sides], axis=0)
+
+    def column(held, hp):
+        return [
+            jnp.sum(jnp.where(head_lane == 2 * hp + i, held, 0.0), axis=-1, keepdims=True)
+            for i in range(2)
+        ]
+
+    near_row = lax.broadcasted_iota(jnp.int32, (4 * ROWS, 1), 0)
+    near_bias = jnp.where(near_row < 2 * ROWS, listed_by(s - 1), listed_by(s + 1))
+
+    def near(hp, carry):
+        query_four = both_sides(qkv, cols_of(hp, 0))
+        scores = dot_nt(query_four, qkv[own, cols_of(hp, 1)]) * SCALE + near_bias
+        totals = jnp.concatenate(column(tot_got[0], hp) + column(tot_got[1], hp), axis=0)
+        near_probs[hp] = jnp.exp(scores) / totals
+        return carry
+
+    arrive(tot_halo)
+    lax.fori_loop(0, PAIRS, near, 0)
 
     def pairs_to(k):
         return remote(
@@ -343,9 +400,6 @@
         o = lax.rem(f + k, frames)
         return remote(usend.at[k - 1], ugot.at[o], us.at[k - 1], ur.at[o], {"frame": o})
 
-    for k in range(1, frames):
-        to_frame(k).start()
-
     hot = (
         lax.broadcasted_iota(jnp.int32, (D, 128), 0) // HD
         == lax.broadcasted_iota(jnp.int32, (D, 128), 1)
@@ -371,7 +425,8 @@
     expos = [jnp.exp(score)]
     prob_grads = [prob_grad]
     for k in range(1, frames):
-        from_frame(k).wait_recv()
+        from_frame(k, 0).wait_recv()
+        from_frame(k, 1).wait_recv()
         o = lax.rem(f + k, frames)
         score, prob_grad = pair_terms(tgot[o])
         expos.append(jnp.exp(score + jnp.where(o < f, 0.0, FAR).astype(F32)))
@@ -422,37 +477,46 @@
         cot_ref[...].astype(F32) + rms_back(stream[...].astype(F32), acc[...])
     ).astype(BF16)
 
-    backward(rows_a, pl.ds(3 * D, D), 0, into(big))
+    def put_ga(at, value):
+        ga_win[own, pl.ds(at, TILE)] = value.astype(BF16)
+
+    backward(rows_a, pl.ds(3 * D, D), 0, put_ga)
+    leave(ga_halo)
+    dlt[...] = per_head(ga_win[own, :].astype(F32) * att[...].astype(F32))
+    leave(dlt_halo)
 
     def attend_back(hp, carry):
-        cols = pl.ds(pl.multiple_of(hp * 128, 128), 128)
-        vcols = pl.ds(pl.multiple_of(D + hp * 128, 128), 128)
-        key = kv_win[:, cols]
-        grad_two = stacked(big[:, cols])
-        query_two = stacked(q_buf[:, cols])
+        cols = cols_of(hp, 0)
+        grad_two = stacked(ga_win[own, cols])
         weight = probs[hp]
-        grad_prob = dot_nt(grad_two, kv_win[:, vcols])
-        held = att[:, cols].astype(F32)
-        row_delta = jnp.sum(
-            grad_two.astype(F32) * jnp.concatenate([held, held], axis=0), axis=-1, keepdims=True
-        )
+        grad_prob = dot_nt(grad_two, qkv[:, cols_of(hp, 2)])
+        row_delta = jnp.concatenate(column(dlt[...], hp), axis=0)
         score_grad = (weight * (grad_prob - row_delta)).astype(BF16)
-        grads[:, cols] = (joined(dot(score_grad, key)) * SCALE).astype(BF16)
-        key_part = dot_tn(score_grad, query_two) * SCALE
-        value_part = dot_tn(weight.astype(BF16), grad_two)
-        for part, at in ((key_part, cols), (value_part, vcols)):
-            gsend[0, :, at] = part[:ROWS].astype(BF16)
-            gown[:, at] = part[ROWS : 2 * ROWS]
-            gsend[1, :, at] = part[2 * ROWS :].astype(BF16)
+        grads[:, cols] = (joined(dot(score_grad, qkv[:, cols_of(hp, 1)])) * SCALE).astype(BF16)
+        middle = slice(ROWS, 2 * ROWS)
+        gown[:, cols] = dot_tn(score_grad[:, middle], stacked(qkv[own, cols]))
+        gown[:, cols_of(hp, 1)] = dot_tn(weight[:, middle].astype(BF16), grad_two)
         return carry
 
     lax.fori_loop(0, PAIRS, attend_back, 0)
-    each_way(lambda way: back_halo[way].start())
     backward(grads.at[:, pl.ds(0, D)], pl.ds(0, D), 0, into(acc))
-    each_way(lambda way: back_halo[1 - way].wait_recv())
-    grads[:, D : 3 * D] = (
-        gown[...] + ggot[0].astype(F32) + ggot[1].astype(F32)
-    ).astype(BF16)
+    arrive(ga_halo)
+    arrive(dlt_halo)
+
+    def near_back(hp, carry):
+        cols = cols_of(hp, 0)
+        grad_four = both_sides(ga_win, cols)
+        weight = near_probs[hp]
+        grad_prob = dot_nt(grad_four, qkv[own, cols_of(hp, 2)])
+        row_delta = jnp.concatenate(column(dlt_got[0], hp) + column(dlt_got[1], hp), axis=0)
+        score_grad = (weight * (grad_prob - row_delta)).astype(BF16)
+        key_grad = gown[:, cols] + dot_tn(score_grad, both_sides(qkv, cols))
+        value_grad = gown[:, cols_of(hp, 1)] + dot_tn(weight.astype(BF16), grad_four)
+        grads[:, cols_of(hp, 1)] = (key_grad * SCALE).astype(BF16)
+        grads[:, cols_of(hp, 2)] = value_grad.astype(BF16)
+        return carry
+
+    lax.fori_loop(0, PAIRS, near_back, 0)
 
     def put_more(at, value):
         cols = pl.ds(at, TILE)
@@ -463,10 +527,11 @@
         rows_a[...].astype(F32) + rms_back(x_ref[...].astype(F32), acc[...])
     ).astype(BF16)
 
-    each_way(lambda way: halo[way].wait_send())
-    each_way(lambda way: back_halo[way].wait_send())
+    for copies in (x_halo, tot_halo, ga_halo, dlt_halo):
+        each_way(lambda way: copies[way].wait_send())
     for k in range(1, frames):
-        to_frame(k).wait_send()
+        for half in range(2):
+            to_frame(k, half).wait_send()
         pairs_to(k).wait_send()
     if gathers:
         gather.close(0)
@@ -489,11 +554,12 @@
         out_specs=[vmem, vmem],
         scratch_shapes=[
             pltpu.VMEM((2, D, 4 * D), BF16),
-            pltpu.VMEM((ROWS, D), BF16),
-            pltpu.VMEM((3 * ROWS, 2 * D), BF16),
+            pltpu.VMEM((3 * ROWS, D), BF16),
+            pltpu.VMEM((3 * ROWS, D), BF16),
+            pltpu.VMEM((3 * ROWS, 3 * D), BF16),
             pltpu.VMEM((ROWS, D), BF16),
             pltpu.VMEM((PAIRS, 2 * ROWS, 3 * ROWS), F32),
-            pltpu.VMEM((ROWS, D), BF16),
+            pltpu.VMEM((PAIRS, 4 * ROWS, ROWS), F32),
             pltpu.VMEM((ROWS, D), BF16),
             pltpu.VMEM((ROWS, D), BF16),
             pltpu.VMEM((2,) + wide, BF16),
@@ -503,14 +569,17 @@
             pltpu.VMEM((ROWS, D), BF16),
             pltpu.VMEM((ROWS, 3 * D), BF16),
             pltpu.VMEM(wide, F32),
-            pltpu.VMEM((2,) + wide, BF16),
-            pltpu.VMEM((2,) + wide, BF16),
+            pltpu.VMEM((3 * ROWS, D), BF16),
+            pltpu.VMEM((ROWS, 128), F32),
+            pltpu.VMEM((2, ROWS, 128), F32),
+            pltpu.VMEM((ROWS, 128), F32),
+            pltpu.VMEM((2, ROWS, 128), F32),
             pltpu.VMEM((ROWS, D), F32),
             dma((4,)),
             dma((2, 2, 4)), dma((2, 4)), dma((2, 4)), dma((2, 4)),
             dma((2, 8)), dma((2, 8)), dma((2, 8)), dma((2, 8)),
-            dma((2,)), dma((2,)), dma((2,)), dma((2,)),
-            dma((frames - 1,)), dma((frames,)), dma((frames - 1,)), dma((frames,)),
+            *[dma((2,))] * 8,
+            dma((frames - 1, 2)), dma((frames, 2)), dma((frames - 1,)), dma((frames,)),
         ],
         compiler_params=pltpu.CompilerParams(
             collective_id=0, has_side_effects=True, vmem_limit_bytes=56 * 1024 * 1024

time: 118 us -> 97.9 us (0.83)
  Pallas kernels: 113 us -> 92.5 us
    pallas_call x1, Pallas kernels: 113 us -> 92.5 us  [local(): pl.pallas_call(functools.partial(kernel, frames, count, gathers), out_sha...]
where the time goes in v2:
time: 97.9 us; the launch traced here: 96.8 us
  Pallas kernels  92.5 us (94%)
  local copies, waits for them, and re-layouts  3.68 us (4%)
    pallas_call x1, Pallas kernels, local(): pl.pallas_call(functools.partial(kernel, frames, count, gathers), out_sha...  92.5 us
    unnamed x7, local copies, waits for them, and re-layouts  3.68 us

profile of v2, /device:TPU:3, one launch (start us, length us, event | category | flops | bytes accessed | tf_op | source)
XLA Modules:
  0.0 96.8 jit_solution(11921604321626148896)
XLA Ops:
  0.6 0.0 copy-start.1
  0.6 0.7 copy-done.1
  1.3 0.7 copy.9.nb_ref
  2.0 92.5 %shard_map.86 = (bf16[128,768]{1,0:T(8,128)(2,1)}, bf16[128,768]{1,0:T(8,128)(2,1)}) custom-call(bf16[128,768]{1,0:T(8,128)(2,1)} %bitcast.4, bf16[128,768]{1,0:T(8,128)(2,1)} %bitcast.5, bf16[96,2304]{1,0:T(8,128)(2,1)} %wqs_ref.1, bf16[96,768]{1,0:T(8,128)(2,1)} %wos_ref.1, bf16[96,2304]{1,0:T(8,128)(2,1)} %wqt_ref.1, bf16[96,768]{1,0:T(8,128)(2,1)} %wot_ref.1, ...), custom_call_target="tpu_custom_call" | custom-call | tf_op jit(solution)/shard_map/pallas_call | solution.py:550
  94.5 0.0 copy-start
  94.5 1.7 %copy.12 = bf16[1,128,768]{2,1,0:T(8,128)(2,1)} copy(bf16[1,128,768]{2,1,0:T(8,128)(2,1)} %bitcast.7) | data formatting | bytes 393216
  96.1 0.0 copy-done
  96.1 0.7 copy.13
Async XLA Ops:
  0.6 0.7 copy-start.1
  94.5 1.7 %copy-start = (bf16[128,768]{1,0:T(8,128)(2,1)S(1)}, bf16[128,768]{1,0:T(8,128)(2,1)}, u32[]{:S(2)}) copy-start(bf16[128,768]{1,0:T(8,128)(2,1)} %get-tuple-element.5) | copy-start | bytes 589828

commit v3 on v2

--- a/solution.py
+++ b/solution.py
@@ -208,20 +208,12 @@
         return jnp.where(first, both[:ROWS], both[ROWS:])
 
     def forward(rows, group, col, width, put):
-        def body(i, carry):
-            at = pl.multiple_of(i * TILE, TILE)
+        for at in range(0, width, TILE):
             put(at, dot(rows[...], weights[group, :, pl.ds(col + at, TILE)]))
-            return carry
-
-        lax.fori_loop(0, width // TILE, body, 0)
 
     def backward(rows, cols, group, put):
-        def body(i, carry):
-            at = pl.multiple_of(i * TILE, TILE)
+        for at in range(0, D, TILE):
             put(at, dot_nt(rows[...], weights[group, pl.ds(at, TILE), cols]))
-            return carry
-
-        lax.fori_loop(0, D // TILE, body, 0)
 
     def into(ref, col=0):
         def put(at, value):
@@ -264,11 +256,10 @@
             tot_got[way] = jnp.ones((ROWS, 128), F32)
             dlt_got[way] = jnp.zeros((ROWS, 128), F32)
 
+    pl.semaphore_wait(barrier, len(peers))
+    leave(x_halo)
     for load in loads:
         load.wait()
-    pl.semaphore_wait(barrier, len(peers))
-
-    leave(x_halo)
     gather = Gather(weights, (zs, zr, xs, xr, ys, yr, cs, cr)) if gathers else None
 
     def pass_on(*steps):
@@ -304,7 +295,7 @@
     head_lane = lax.broadcasted_iota(jnp.int32, (1, 128), 1)
 
     def cols_of(hp, part):
-        return pl.ds(pl.multiple_of(part * D + hp * 128, 128), 128)
+        return pl.ds(part * D + hp * 128, 128)
 
     def attend(hp, totals):
         cols = cols_of(hp, 0)
@@ -317,7 +308,10 @@
         totals = jnp.where(head_lane == 2 * hp, total[:ROWS], totals)
         return jnp.where(head_lane == 2 * hp + 1, total[ROWS:], totals)
 
-    tot[...] = lax.fori_loop(0, PAIRS, attend, jnp.ones((ROWS, 128), F32))
+    totals = jnp.ones((ROWS, 128), F32)
+    for hp in range(PAIRS):
+        totals = attend(hp, totals)
+    tot[...] = totals
     leave(tot_halo)
 
     if gathers:
@@ -381,15 +375,15 @@
     near_row = lax.broadcasted_iota(jnp.int32, (4 * ROWS, 1), 0)
     near_bias = jnp.where(near_row < 2 * ROWS, listed_by(s - 1), listed_by(s + 1))
 
-    def near(hp, carry):
+    def near(hp):
         query_four = both_sides(qkv, cols_of(hp, 0))
         scores = dot_nt(query_four, qkv[own, cols_of(hp, 1)]) * SCALE + near_bias
         totals = jnp.concatenate(column(tot_got[0], hp) + column(tot_got[1], hp), axis=0)
         near_probs[hp] = jnp.exp(scores) / totals
-        return carry
 
     arrive(tot_halo)
-    lax.fori_loop(0, PAIRS, near, 0)
+    for hp in range(PAIRS):
+        near(hp)
 
     def pairs_to(k):
         return remote(
@@ -485,7 +479,7 @@
     dlt[...] = per_head(ga_win[own, :].astype(F32) * att[...].astype(F32))
     leave(dlt_halo)
 
-    def attend_back(hp, carry):
+    def attend_back(hp):
         cols = cols_of(hp, 0)
         grad_two = stacked(ga_win[own, cols])
         weight = probs[hp]
@@ -496,14 +490,14 @@
         middle = slice(ROWS, 2 * ROWS)
         gown[:, cols] = dot_tn(score_grad[:, middle], stacked(qkv[own, cols]))
         gown[:, cols_of(hp, 1)] = dot_tn(weight[:, middle].astype(BF16), grad_two)
-        return carry
-
-    lax.fori_loop(0, PAIRS, attend_back, 0)
+
+    for hp in range(PAIRS):
+        attend_back(hp)
     backward(grads.at[:, pl.ds(0, D)], pl.ds(0, D), 0, into(acc))
     arrive(ga_halo)
     arrive(dlt_halo)
 
-    def near_back(hp, carry):
+    def near_back(hp):
         cols = cols_of(hp, 0)
         grad_four = both_sides(ga_win, cols)
         weight = near_probs[hp]
@@ -514,9 +508,9 @@
         value_grad = gown[:, cols_of(hp, 1)] + dot_tn(weight.astype(BF16), grad_four)
         grads[:, cols_of(hp, 1)] = (key_grad * SCALE).astype(BF16)
         grads[:, cols_of(hp, 2)] = value_grad.astype(BF16)
-        return carry
-
-    lax.fori_loop(0, PAIRS, near_back, 0)
+
+    for hp in range(PAIRS):
+        near_back(hp)
 
     def put_more(at, value):
         cols = pl.ds(at, TILE)

time: 97.9 us -> 94.5 us (0.965)
  Pallas kernels: 92.5 us -> 90 us
    pallas_call x1, Pallas kernels: 92.5 us -> 90 us  [local(): pl.pallas_call(functools.partial(kernel, frames, count, gathers), out_sha...]
where the time goes in v3:
time: 94.5 us; the launch traced here: 94.3 us
  Pallas kernels  90 us (95%)
  local copies, waits for them, and re-layouts  3.68 us (4%)
    pallas_call x1, Pallas kernels, local(): pl.pallas_call(functools.partial(kernel, frames, count, gathers), out_sha...  90 us
    unnamed x7, local copies, waits for them, and re-layouts  3.68 us

profile of v3, /device:TPU:3, one launch (start us, length us, event | category | flops | bytes accessed | tf_op | source)
XLA Modules:
  0.0 94.3 jit_solution(8913180707076287582)
XLA Ops:
  0.6 0.0 copy-start.1
  0.6 0.7 copy-done.1
  1.3 0.7 copy.9.nb_ref
  2.0 90.0 %shard_map.86 = (bf16[128,768]{1,0:T(8,128)(2,1)}, bf16[128,768]{1,0:T(8,128)(2,1)}) custom-call(bf16[128,768]{1,0:T(8,128)(2,1)} %bitcast.4, bf16[128,768]{1,0:T(8,128)(2,1)} %bitcast.5, bf16[96,2304]{1,0:T(8,128)(2,1)} %wqs_ref.1, bf16[96,768]{1,0:T(8,128)(2,1)} %wos_ref.1, bf16[96,2304]{1,0:T(8,128)(2,1)} %wqt_ref.1, bf16[96,768]{1,0:T(8,128)(2,1)} %wot_ref.1, ...), custom_call_target="tpu_custom_call" | custom-call | tf_op jit(solution)/shard_map/pallas_call | solution.py:544
  91.9 0.0 copy-start
  92.0 1.7 %copy.12 = bf16[1,128,768]{2,1,0:T(8,128)(2,1)} copy(bf16[1,128,768]{2,1,0:T(8,128)(2,1)} %bitcast.7) | data formatting | bytes 393216
  93.6 0.0 copy-done
  93.6 0.7 copy.13
Async XLA Ops:
  0.6 0.7 copy-start.1
  91.9 1.7 %copy-start = (bf16[128,768]{1,0:T(8,128)(2,1)S(1)}, bf16[128,768]{1,0:T(8,128)(2,1)}, u32[]{:S(2)}) copy-start(bf16[128,768]{1,0:T(8,128)(2,1)} %get-tuple-element.5) | copy-start | bytes 589828

commit v4 on v3

--- a/solution.py
+++ b/solution.py
@@ -169,8 +169,8 @@
     frames, count, gathers,
     x_ref, cot_ref, wqs_ref, wos_ref, wqt_ref, wot_ref, nb_ref,
     out_ref, grad_ref,
-    weights, x_win, normed, qkv, att, probs, near_probs, stream, rows_a, tsend, tgot, usend, ugot,
-    attn_t, grads, gown, ga_win, tot, tot_got, dlt, dlt_got, acc,
+    weights, x_win, normed, qkv, att, probs, near_probs, streams, cots, normed_t, qkv_t, ga_t, shares_t, score_t,
+    rows_a, attn_t, grads, gown, ga_win, tot, tot_got, dlt, dlt_got, acc,
     load_sem, zs, zr, xs, xr, ys, yr, cs, cr, hs, hr, bs, br, ds, dr, es, er, ts, tr, us, ur,
 ):
     s = lax.axis_index("space")
@@ -246,6 +246,21 @@
     tot_halo = two_ways(tot, [tot_got.at[way] for way in range(2)], ds, dr)
     dlt_halo = two_ways(dlt, [dlt_got.at[way] for way in range(2)], es, er)
 
+    mine = pl.ds(pl.multiple_of(f * ROWS, ROWS), ROWS)
+
+    def frame_copies(src, held, send, recv):
+        out, got = [], []
+        for k in range(1, frames):
+            o = lax.rem(f + k, frames)
+            theirs = pl.ds(pl.multiple_of(o * ROWS, ROWS), ROWS)
+            where = {"frame": o}
+            out.append(remote(src, held.at[mine, :], send.at[k - 1], recv.at[f], where))
+            got.append(remote(src, held.at[theirs, :], send.at[k - 1], recv.at[o], where))
+        return out, got
+
+    cot_out, cot_got = frame_copies(cot_ref, cots, ts, tr)
+    stream_out, stream_got = frame_copies(streams.at[mine, :], streams, us, ur)
+    cots[mine, :] = cot_ref[...]
     x_win[own, :] = x_ref[...]
     for way in range(2):
 
@@ -253,11 +268,13 @@
         def _():
             x_win[sides[way], :] = jnp.zeros((ROWS, D), BF16)
             ga_win[sides[way], :] = jnp.zeros((ROWS, D), BF16)
-            tot_got[way] = jnp.ones((ROWS, 128), F32)
-            dlt_got[way] = jnp.zeros((ROWS, 128), F32)
+            tot_got[way] = jnp.ones((16, 128), F32)
+            dlt_got[way] = jnp.zeros((16, 128), F32)
 
     pl.semaphore_wait(barrier, len(peers))
     leave(x_halo)
+    for copy in cot_out:
+        copy.start()
     for load in loads:
         load.wait()
     gather = Gather(weights, (zs, zr, xs, xr, ys, yr, cs, cr)) if gathers else None
@@ -268,8 +285,8 @@
                 getattr(gather, name)(*where)
 
     pass_on(
-        ("open", 0), ("open", 1),
-        ("z_step", 0, 1), ("x_step", 0, 0), ("z_step", 0, 2), ("x_step", 0, 1), ("z_step", 0, 3),
+        ("open", 0),
+        ("z_step", 0, 1), ("x_step", 0, 0), ("z_step", 0, 2), ("open", 1), ("x_step", 0, 1), ("z_step", 0, 3),
         ("x_step", 0, 2), ("z_step", 1, 1), ("x_step", 0, 3),
     )
     arrive(x_halo)
@@ -311,50 +328,14 @@
     totals = jnp.ones((ROWS, 128), F32)
     for hp in range(PAIRS):
         totals = attend(hp, totals)
-    tot[...] = totals
+    tot[...] = totals.T[:16]
     leave(tot_halo)
 
-    if gathers:
-        gather.y_stage(1)
-
     forward(att, 0, 3 * D, D, into(acc))
-    stream[...] = (x_ref[...].astype(F32) + acc[...]).astype(BF16)
-    values = stream[...].astype(F32)
-    rows_a[...] = (values * rms_factor(values)).astype(BF16)
-
-    if gathers:
-        gather.c_stage(1)
-
-    def frame_copy(k, half, o, slot):
-        cols = pl.ds(half * D, D)
-        return remote(
-            tsend.at[(f + k) // frames, :, cols], tgot.at[slot, :, cols],
-            ts.at[k - 1, half], tr.at[slot, half], {"frame": o},
-        )
-
-    def to_frame(k, half):
-        return frame_copy(k, half, lax.rem(f + k, frames), f)
-
-    def from_frame(k, half):
-        o = lax.rem(f + k, frames)
-        return frame_copy(k, half, o, o)
-
-    def to_later(half):
-        for k in range(1, frames):
-            pl.when(f + k < frames)(lambda: to_frame(k, half).start())
-
-    def to_earlier(half):
-        for k in range(1, frames):
-            pl.when(f + k >= frames)(lambda: to_frame(k, half).start())
-
-    forward(rows_a, 1, D, D, into(tsend.at[0]))
-    to_later(0)
-    forward(rows_a, 1, 2 * D, D, into(tsend.at[0], D))
-    to_later(1)
-    forward(rows_a, 1, 0, D, into(tsend.at[1]))
-    to_earlier(0)
-    backward(cot_ref, pl.ds(3 * D, D), 1, into(tsend.at[1], D))
-    to_earlier(1)
+    streams[mine, :] = (x_ref[...].astype(F32) + acc[...]).astype(BF16)
+    for copy in stream_out:
+        copy.start()
+    pass_on(("y_stage", 1))
 
     def listed_by(block):
         row = jnp.clip(block, 0, count - 1)
@@ -372,27 +353,30 @@
             for i in range(2)
         ]
 
-    near_row = lax.broadcasted_iota(jnp.int32, (4 * ROWS, 1), 0)
+    def near_lanes(held, hp):
+        return jnp.concatenate(
+            [held[way, 2 * hp + i : 2 * hp + i + 1, :] for way in range(2) for i in range(2)], axis=1
+        )
+
+    near_row = lax.broadcasted_iota(jnp.int32, (1, 4 * ROWS), 1)
     near_bias = jnp.where(near_row < 2 * ROWS, listed_by(s - 1), listed_by(s + 1))
 
     def near(hp):
         query_four = both_sides(qkv, cols_of(hp, 0))
-        scores = dot_nt(query_four, qkv[own, cols_of(hp, 1)]) * SCALE + near_bias
-        totals = jnp.concatenate(column(tot_got[0], hp) + column(tot_got[1], hp), axis=0)
-        near_probs[hp] = jnp.exp(scores) / totals
+        scores = dot_nt(qkv[own, cols_of(hp, 1)], query_four) * SCALE + near_bias
+        near_probs[hp] = jnp.exp(scores) / near_lanes(tot_got, hp)
 
     arrive(tot_halo)
     for hp in range(PAIRS):
         near(hp)
 
-    def pairs_to(k):
-        return remote(
-            usend.at[k - 1], ugot.at[f], us.at[k - 1], ur.at[f], {"frame": lax.rem(f + k, frames)}
-        )
-
-    def pairs_from(k):
-        o = lax.rem(f + k, frames)
-        return remote(usend.at[k - 1], ugot.at[o], us.at[k - 1], ur.at[o], {"frame": o})
+    pass_on(("c_stage", 1))
+    for copy in stream_got + cot_got:
+        copy.wait_recv()
+    values = streams[...].astype(F32)
+    normed_t[...] = (values * rms_factor(values)).astype(BF16)
+    forward(normed_t, 1, 0, 3 * D, into(qkv_t))
+    backward(cots, pl.ds(3 * D, D), 1, into(ga_t))
 
     hot = (
         lax.broadcasted_iota(jnp.int32, (D, 128), 0) // HD
@@ -407,68 +391,52 @@
     def spread(heads):
         return dot_nt(heads, hot)
 
-    query = tsend[1, :, 0:D].astype(F32)
-    grad_att = tsend[1, :, D : 2 * D].astype(F32)
-
-    def pair_terms(held):
-        key = held[:, 0:D].astype(F32)
-        value = held[:, D : 2 * D].astype(F32)
-        return per_head(query * key) * SCALE, per_head(grad_att * value)
-
-    score, prob_grad = pair_terms(tsend[0])
-    expos = [jnp.exp(score)]
-    prob_grads = [prob_grad]
-    for k in range(1, frames):
-        from_frame(k, 0).wait_recv()
-        from_frame(k, 1).wait_recv()
-        o = lax.rem(f + k, frames)
-        score, prob_grad = pair_terms(tgot[o])
-        expos.append(jnp.exp(score + jnp.where(o < f, 0.0, FAR).astype(F32)))
-        prob_grads.append(prob_grad)
-    total = sum(expos[1:], expos[0])
-    shares = [expo / total for expo in expos]
-    rounded = [share.astype(BF16) for share in shares]
-
-    def held_at(k):
-        return tsend[0] if k == 0 else tgot[lax.rem(f + k, frames)]
-
-    update = spread(rounded[0]) * held_at(0)[:, D : 2 * D].astype(F32)
-    for k in range(1, frames):
-        update = update + spread(rounded[k]) * held_at(k)[:, D : 2 * D].astype(F32)
-    attn_t[...] = update.astype(BF16)
-    delta = per_head(grad_att * attn_t[...].astype(F32))
-    score_grads = [
-        (share * (grad - delta)).astype(BF16) for share, grad in zip(shares, prob_grads)
-    ]
-    for k in range(1, frames):
-        usend[k - 1, :, 0:128] = rounded[k]
-        usend[k - 1, :, 128:256] = score_grads[k]
-        pairs_to(k).start()
+    def frame_rows(i):
+        return pl.ds(i * ROWS, ROWS)
+
+    def part(i, which):
+        return qkv_t[frame_rows(i), which * D : (which + 1) * D].astype(F32)
+
+    for i in range(frames):
+        query = part(i, 0)
+        grad_att = ga_t[frame_rows(i), :].astype(F32)
+        expos = [jnp.exp(per_head(query * part(g, 1)) * SCALE) for g in range(i + 1)]
+        prob_grads = [per_head(grad_att * part(g, 2)) for g in range(i + 1)]
+        total = sum(expos[1:], expos[0])
+        shares = [expo / total for expo in expos]
+        rounded = [share.astype(BF16) for share in shares]
+        terms = [prob.astype(F32) * grad for prob, grad in zip(rounded, prob_grads)]
+        delta = sum(terms[1:], terms[0])
+        for g in range(frames):
+            if g <= i:
+                shares_t[i, g] = rounded[g]
+                score_t[i, g] = (shares[g] * (prob_grads[g] - delta)).astype(BF16)
+            else:
+                shares_t[i, g] = jnp.zeros((ROWS, 128), BF16)
+                score_t[i, g] = jnp.zeros((ROWS, 128), BF16)
+
+    def over_frames(term):
+        total = term(0)
+        for i in range(1, frames):
+            total = total + term(i)
+        return total
+
+    attn_t[...] = over_frames(lambda g: spread(shares_t[f, g]) * part(g, 2)).astype(BF16)
+    grads[:, 0:D] = (over_frames(lambda g: spread(score_t[f, g]) * part(g, 1)) * SCALE).astype(BF16)
+    grads[:, D : 2 * D] = (
+        over_frames(lambda i: spread(score_t[i, f]) * part(i, 0)) * SCALE
+    ).astype(BF16)
+    grads[:, 2 * D : 3 * D] = over_frames(
+        lambda i: spread(shares_t[i, f]) * ga_t[frame_rows(i), :].astype(F32)
+    ).astype(BF16)
 
     def put_out(at, value):
         cols = pl.ds(at, TILE)
-        out_ref[:, cols] = (stream[:, cols].astype(F32) + value).astype(BF16)
-
-    forward(attn_t, 1, 3 * D, D, put_out)
-
-    update = spread(score_grads[0]) * held_at(0)[:, 0:D].astype(F32)
-    for k in range(1, frames):
-        update = update + spread(score_grads[k]) * held_at(k)[:, 0:D].astype(F32)
-    grads[:, 0:D] = (update * SCALE).astype(BF16)
-
-    key_grad = spread(score_grads[0]) * query
-    value_grad = spread(rounded[0]) * grad_att
-    for k in range(1, frames):
-        pairs_from(k).wait_recv()
-        o = lax.rem(f + k, frames)
-        key_grad = key_grad + spread(ugot[o, :, 128:256]) * tgot[o, :, 0:D].astype(F32)
-        value_grad = value_grad + spread(ugot[o, :, 0:128]) * tgot[o, :, D : 2 * D].astype(F32)
-    grads[:, D : 2 * D] = (key_grad * SCALE).astype(BF16)
-    grads[:, 2 * D : 3 * D] = value_grad.astype(BF16)
+        out_ref[:, cols] = (streams[mine, cols].astype(F32) + value).astype(BF16)
 
     backward(grads, pl.ds(0, 3 * D), 1, into(acc))
     rows_a[...] = (
-        cot_ref[...].astype(F32) + rms_back(stream[...].astype(F32), acc[...])
+        cot_ref[...].astype(F32) + rms_back(streams[mine, :].astype(F32), acc[...])
     ).astype(BF16)
 
     def put_ga(at, value):
@@ -476,7 +444,8 @@
 
     backward(rows_a, pl.ds(3 * D, D), 0, put_ga)
     leave(ga_halo)
-    dlt[...] = per_head(ga_win[own, :].astype(F32) * att[...].astype(F32))
+    deltas = per_head(ga_win[own, :].astype(F32) * att[...].astype(F32))
+    dlt[...] = deltas.T[:16]
     leave(dlt_halo)
 
     def attend_back(hp):
@@ -484,7 +453,7 @@
         grad_two = stacked(ga_win[own, cols])
         weight = probs[hp]
         grad_prob = dot_nt(grad_two, qkv[:, cols_of(hp, 2)])
-        row_delta = jnp.concatenate(column(dlt[...], hp), axis=0)
+        row_delta = jnp.concatenate(column(deltas, hp), axis=0)
         score_grad = (weight * (grad_prob - row_delta)).astype(BF16)
         grads[:, cols] = (joined(dot(score_grad, qkv[:, cols_of(hp, 1)])) * SCALE).astype(BF16)
         middle = slice(ROWS, 2 * ROWS)
@@ -493,6 +462,7 @@
 
     for hp in range(PAIRS):
         attend_back(hp)
+    forward(attn_t, 1, 3 * D, D, put_out)
     backward(grads.at[:, pl.ds(0, D)], pl.ds(0, D), 0, into(acc))
     arrive(ga_halo)
     arrive(dlt_halo)
@@ -501,11 +471,10 @@
         cols = cols_of(hp, 0)
         grad_four = both_sides(ga_win, cols)
         weight = near_probs[hp]
-        grad_prob = dot_nt(grad_four, qkv[own, cols_of(hp, 2)])
-        row_delta = jnp.concatenate(column(dlt_got[0], hp) + column(dlt_got[1], hp), axis=0)
-        score_grad = (weight * (grad_prob - row_delta)).astype(BF16)
-        key_grad = gown[:, cols] + dot_tn(score_grad, both_sides(qkv, cols))
-        value_grad = gown[:, cols_of(hp, 1)] + dot_tn(weight.astype(BF16), grad_four)
+        grad_prob = dot_nt(qkv[own, cols_of(hp, 2)], grad_four)
+        score_grad = (weight * (grad_prob - near_lanes(dlt_got, hp))).astype(BF16)
+        key_grad = gown[:, cols] + dot(score_grad, both_sides(qkv, cols))
+        value_grad = gown[:, cols_of(hp, 1)] + dot(weight.astype(BF16), grad_four)
         grads[:, cols_of(hp, 1)] = (key_grad * SCALE).astype(BF16)
         grads[:, cols_of(hp, 2)] = value_grad.astype(BF16)
 
@@ -523,10 +492,8 @@
 
     for copies in (x_halo, tot_halo, ga_halo, dlt_halo):
         each_way(lambda way: copies[way].wait_send())
-    for k in range(1, frames):
-        for half in range(2):
-            to_frame(k, half).wait_send()
-        pairs_to(k).wait_send()
+    for copy in cot_out + stream_out:
+        copy.wait_send()
     if gathers:
         gather.close(0)
         gather.close(1)
@@ -553,27 +520,23 @@
             pltpu.VMEM((3 * ROWS, 3 * D), BF16),
             pltpu.VMEM((ROWS, D), BF16),
             pltpu.VMEM((PAIRS, 2 * ROWS, 3 * ROWS), F32),
-            pltpu.VMEM((PAIRS, 4 * ROWS, ROWS), F32),
+            pltpu.VMEM((PAIRS, ROWS, 4 * ROWS), F32),
+            *[pltpu.VMEM((frames * ROWS, D), BF16)] * 3,
+            pltpu.VMEM((frames * ROWS, 3 * D), BF16),
+            pltpu.VMEM((frames * ROWS, D), BF16),
+            *[pltpu.VMEM((frames, frames, ROWS, 128), BF16)] * 2,
             pltpu.VMEM((ROWS, D), BF16),
-            pltpu.VMEM((ROWS, D), BF16),
-            pltpu.VMEM((2,) + wide, BF16),
-            pltpu.VMEM((frames,) + wide, BF16),
-            pltpu.VMEM((frames - 1, ROWS, 256), BF16),
-            pltpu.VMEM((frames, ROWS, 256), BF16),
             pltpu.VMEM((ROWS, D), BF16),
             pltpu.VMEM((ROWS, 3 * D), BF16),
             pltpu.VMEM(wide, F32),
             pltpu.VMEM((3 * ROWS, D), BF16),
-            pltpu.VMEM((ROWS, 128), F32),
-            pltpu.VMEM((2, ROWS, 128), F32),
-            pltpu.VMEM((ROWS, 128), F32),
-            pltpu.VMEM((2, ROWS, 128), F32),
+            *[pltpu.VMEM((16, 128), F32), pltpu.VMEM((2, 16, 128), F32)] * 2,
             pltpu.VMEM((ROWS, D), F32),
             dma((4,)),
             dma((2, 2, 4)), dma((2, 4)), dma((2, 4)), dma((2, 4)),
             dma((2, 8)), dma((2, 8)), dma((2, 8)), dma((2, 8)),
             *[dma((2,))] * 8,
-            dma((frames - 1, 2)), dma((frames, 2)), dma((frames - 1,)), dma((frames,)),
+            *[dma((frames - 1,)), dma((frames,))] * 2,
         ],
         compiler_params=pltpu.CompilerParams(
             collective_id=0, has_side_effects=True, vmem_limit_bytes=56 * 1024 * 1024

time: 94.5 us -> 78.8 us (0.83)
  Pallas kernels: 90 us -> 74 us
    pallas_call x1, Pallas kernels: 90 us -> 74 us  [local(): pl.pallas_call(functools.partial(kernel, frames, count, gathers), out_sha...]
where the time goes in v4:
time: 78.8 us; the launch traced here: 78.4 us
  Pallas kernels  74 us (94%)
  local copies, waits for them, and re-layouts  3.68 us (5%)
    pallas_call x1, Pallas kernels, local(): pl.pallas_call(functools.partial(kernel, frames, count, gathers), out_sha...  74 us
    unnamed x7, local copies, waits for them, and re-layouts  3.68 us

profile of v4, /device:TPU:3, one launch (start us, length us, event | category | flops | bytes accessed | tf_op | source)
XLA Modules:
  0.0 78.4 jit_solution(4195121129437106517)
XLA Ops:
  0.6 0.0 copy-start.1
  0.6 0.7 copy-done.1
  1.3 0.7 copy.9.nb_ref
  2.0 74.0 %shard_map.86 = (bf16[128,768]{1,0:T(8,128)(2,1)}, bf16[128,768]{1,0:T(8,128)(2,1)}) custom-call(bf16[128,768]{1,0:T(8,128)(2,1)} %bitcast.4, bf16[128,768]{1,0:T(8,128)(2,1)} %bitcast.5, bf16[96,2304]{1,0:T(8,128)(2,1)} %wqs_ref.1, bf16[96,768]{1,0:T(8,128)(2,1)} %wos_ref.1, bf16[96,2304]{1,0:T(8,128)(2,1)} %wqt_ref.1, bf16[96,768]{1,0:T(8,128)(2,1)} %wot_ref.1, ...), custom_call_target="tpu_custom_call" | custom-call | tf_op jit(solution)/shard_map/pallas_call | solution.py:511
  76.0 0.0 copy-start
  76.0 1.7 %copy.12 = bf16[1,128,768]{2,1,0:T(8,128)(2,1)} copy(bf16[1,128,768]{2,1,0:T(8,128)(2,1)} %bitcast.7) | data formatting | bytes 393216
  77.7 0.0 copy-done
  77.7 0.7 copy.13
Async XLA Ops:
  0.6 0.7 copy-start.1
  76.0 1.7 %copy-start = (bf16[128,768]{1,0:T(8,128)(2,1)S(1)}, bf16[128,768]{1,0:T(8,128)(2,1)}, u32[]{:S(2)}) copy-start(bf16[128,768]{1,0:T(8,128)(2,1)} %get-tuple-element.5) | copy-start | bytes 589828

commit v5 on v4

--- a/solution.py
+++ b/solution.py
@@ -59,10 +59,11 @@
 
     def __init__(self, weights, sems):
         self.w = weights
-        self.zs, self.zr, self.xs, self.xr, self.ys, self.yr, self.cs, self.cr = sems
+        self.zs, self.zr, self.xs, self.xr, self.ys, self.yr, self.cs, self.cr, self.ps, self.pr = sems
         self.s = lax.axis_index("space")
         self.z = self.s // self.X
         self.x = self.s % self.X
+        self.pair = self.z + 1 - 2 * (self.z % 2)
         self.odd = lax.axis_index("frame")
         self.c = lax.axis_index("dp")
 
@@ -85,6 +86,11 @@
         partner = self.s + 1 - 2 * self.x
         return remote(ref, ref, self.xs.at[group, at], self.xr.at[group, at], {"space": partner})
 
+    def to_pair(self, group, at):
+        ref = self.main(group, at * self.X + 1 - self.x)
+        where = {"space": self.s + (self.pair - self.z) * self.X}
+        return remote(ref, ref, self.ps.at[group], self.pr.at[group], where)
+
     def along_y(self, group, shard, sending):
         which = self.odd if sending else 1 - self.odd
         ref = self.rows(group, shard, 48 * self.c + 32 * which, 16)
@@ -123,7 +129,7 @@
                 def _():
                     self.along_z(group, step, at).start()
 
-                self.along_x(group, at, self.x).start()
+                pl.when(at != self.pair)(lambda: self.along_x(group, at, self.x).start())
                 self.along_y(group, at * self.X + self.x, True).start()
 
     def x_step(self, group, distance):
@@ -132,7 +138,10 @@
 
             @pl.when((at >= 0) & (at < self.Z))
             def _():
-                self.along_x(group, at, 1 - self.x).wait_recv()
+                pl.when(at != self.pair)(lambda: self.along_x(group, at, 1 - self.x).wait_recv())
+                pl.when(at == self.pair)(lambda: self.to_pair(group, at).wait_recv())
+                if distance == 0:
+                    self.to_pair(group, at).start()
                 self.along_y(group, at * self.X + 1 - self.x, True).start()
 
     def others(self):
@@ -159,7 +168,8 @@
             def _():
                 self.along_z(group, -1, at).wait_send()
 
-            self.along_x(group, at, self.x).wait_send()
+            pl.when(at != self.pair)(lambda: self.along_x(group, at, self.x).wait_send())
+        self.to_pair(group, self.z).wait_send()
         for shard in self.others():
             self.along_y(group, shard, True).wait_send()
             self.across(group, shard, True).wait_send()
@@ -171,7 +181,7 @@
     out_ref, grad_ref,
     weights, x_win, normed, qkv, att, probs, near_probs, streams, cots, normed_t, qkv_t, ga_t, shares_t, score_t,
     rows_a, attn_t, grads, gown, ga_win, tot, tot_got, dlt, dlt_got, acc,
-    load_sem, zs, zr, xs, xr, ys, yr, cs, cr, hs, hr, bs, br, ds, dr, es, er, ts, tr, us, ur,
+    load_sem, zs, zr, xs, xr, ys, yr, cs, cr, ps, pr, hs, hr, bs, br, ds, dr, es, er, ts, tr, us, ur,
 ):
     s = lax.axis_index("space")
     f = lax.axis_index("frame")
@@ -242,7 +252,13 @@
         each_way(lambda way: copies[1 - way].wait_recv())
 
     x_halo = two_ways(x_ref, [x_win.at[side, :] for side in sides], hs, hr)
-    ga_halo = two_ways(ga_win.at[own, :], [ga_win.at[side, :] for side in sides], bs, br)
+    thirds = [pl.ds(at, TILE) for at in range(0, D, TILE)]
+    ga_halo = [
+        two_ways(
+            ga_win.at[own, cols], [ga_win.at[side, cols] for side in sides], bs.at[i], br.at[i]
+        )
+        for i, cols in enumerate(thirds)
+    ]
     tot_halo = two_ways(tot, [tot_got.at[way] for way in range(2)], ds, dr)
     dlt_halo = two_ways(dlt, [dlt_got.at[way] for way in range(2)], es, er)
 
@@ -277,7 +293,7 @@
         copy.start()
     for load in loads:
         load.wait()
-    gather = Gather(weights, (zs, zr, xs, xr, ys, yr, cs, cr)) if gathers else None
+    gather = Gather(weights, (zs, zr, xs, xr, ys, yr, cs, cr, ps, pr)) if gathers else None
 
     def pass_on(*steps):
         if gathers:
@@ -443,10 +459,11 @@
         ga_win[own, pl.ds(at, TILE)] = value.astype(BF16)
 
     backward(rows_a, pl.ds(3 * D, D), 0, put_ga)
-    leave(ga_halo)
     deltas = per_head(ga_win[own, :].astype(F32) * att[...].astype(F32))
     dlt[...] = deltas.T[:16]
     leave(dlt_halo)
+    for copies in ga_halo:
+        leave(copies)
 
     def attend_back(hp):
         cols = cols_of(hp, 0)
@@ -464,7 +481,6 @@
         attend_back(hp)
     forward(attn_t, 1, 3 * D, D, put_out)
     backward(grads.at[:, pl.ds(0, D)], pl.ds(0, D), 0, into(acc))
-    arrive(ga_halo)
     arrive(dlt_halo)
 
     def near_back(hp):
@@ -479,6 +495,8 @@
         grads[:, cols_of(hp, 2)] = value_grad.astype(BF16)
 
     for hp in range(PAIRS):
+        if hp % 2 == 0:
+            arrive(ga_halo[hp // 2])
         near_back(hp)
 
     def put_more(at, value):
@@ -490,7 +508,7 @@
         rows_a[...].astype(F32) + rms_back(x_ref[...].astype(F32), acc[...])
     ).astype(BF16)
 
-    for copies in (x_halo, tot_halo, ga_halo, dlt_halo):
+    for copies in (x_halo, tot_halo, dlt_halo, *ga_halo):
         each_way(lambda way: copies[way].wait_send())
     for copy in cot_out + stream_out:
         copy.wait_send()
@@ -535,7 +553,9 @@
             dma((4,)),
             dma((2, 2, 4)), dma((2, 4)), dma((2, 4)), dma((2, 4)),
             dma((2, 8)), dma((2, 8)), dma((2, 8)), dma((2, 8)),
-            *[dma((2,))] * 8,
+            dma((2,)), dma((2,)), dma((2,)), dma((2,)),
+            *[dma((3, 2))] * 2,
+            *[dma((2,))] * 4,
             *[dma((frames - 1,)), dma((frames,))] * 2,
         ],
         compiler_params=pltpu.CompilerParams(

time: 78.8 us -> 78.4 us (level)
  no operation moved by 1% of the time
where the time goes in v5:
time: 78.4 us; the launch traced here: 78.2 us
  Pallas kernels  73.9 us (94%)
  local copies, waits for them, and re-layouts  3.68 us (5%)
    pallas_call x1, Pallas kernels, local(): pl.pallas_call(functools.partial(kernel, frames, count, gathers), out_sha...  73.9 us
    unnamed x7, local copies, waits for them, and re-layouts  3.68 us

profile of v5, /device:TPU:3, one launch (start us, length us, event | category | flops | bytes accessed | tf_op | source)
XLA Modules:
  0.0 78.2 jit_solution(4841854534760551801)
XLA Ops:
  0.6 0.0 copy-start.1
  0.6 0.7 copy-done.1
  1.3 0.7 copy.9.nb_ref
  2.0 73.9 %shard_map.86 = (bf16[128,768]{1,0:T(8,128)(2,1)}, bf16[128,768]{1,0:T(8,128)(2,1)}) custom-call(bf16[128,768]{1,0:T(8,128)(2,1)} %bitcast.4, bf16[128,768]{1,0:T(8,128)(2,1)} %bitcast.5, bf16[96,2304]{1,0:T(8,128)(2,1)} %wqs_ref.1, bf16[96,768]{1,0:T(8,128)(2,1)} %wos_ref.1, bf16[96,2304]{1,0:T(8,128)(2,1)} %wqt_ref.1, bf16[96,768]{1,0:T(8,128)(2,1)} %wot_ref.1, ...), custom_call_target="tpu_custom_call" | custom-call | tf_op jit(solution)/shard_map/pallas_call | solution.py:529
  75.8 0.0 copy-start
  75.9 1.7 %copy.12 = bf16[1,128,768]{2,1,0:T(8,128)(2,1)} copy(bf16[1,128,768]{2,1,0:T(8,128)(2,1)} %bitcast.7) | data formatting | bytes 393216
  77.5 0.0 copy-done
  77.5 0.7 copy.13
Async XLA Ops:
  0.6 0.7 copy-start.1
  75.8 1.7 %copy-start = (bf16[128,768]{1,0:T(8,128)(2,1)S(1)}, bf16[128,768]{1,0:T(8,128)(2,1)}, u32[]{:S(2)}) copy-start(bf16[128,768]{1,0:T(8,128)(2,1)} %get-tuple-element.5) | copy-start | bytes 589828

commit v6 on v4

--- a/solution.py
+++ b/solution.py
@@ -59,7 +59,7 @@
 
     def __init__(self, weights, sems):
         self.w = weights
-        self.zs, self.zr, self.xs, self.xr, self.ys, self.yr, self.cs, self.cr = sems
+        self.zs, self.zr, self.xs, self.xr, self.ys, self.yr, self.cs, self.cr, self.ps, self.pr = sems
         self.s = lax.axis_index("space")
         self.z = self.s // self.X
         self.x = self.s % self.X
@@ -94,9 +94,16 @@
 
     def across(self, group, shard, sending):
         half = self.c if sending else 1 - self.c
-        ref = self.rows(group, shard, 48 * half, 48)
+        ref = self.rows(group, shard, 48 * half + 16 * self.odd, 32)
         return remote(
             ref, ref, self.cs.at[group, shard], self.cr.at[group, shard], {"dp": 1 - self.c}
+        )
+
+    def across_rest(self, group, shard, sending):
+        half = self.c if sending else 1 - self.c
+        ref = self.rows(group, shard, 48 * half + 32 * (1 - self.odd), 16)
+        return remote(
+            ref, ref, self.ps.at[group, shard], self.pr.at[group, shard], {"dp": 1 - self.c}
         )
 
     def open(self, group):
@@ -125,6 +132,7 @@
 
                 self.along_x(group, at, self.x).start()
                 self.along_y(group, at * self.X + self.x, True).start()
+                self.across(group, at * self.X + self.x, True).start()
 
     def x_step(self, group, distance):
         for step in (1, -1) if distance else (1,):
@@ -134,6 +142,7 @@
             def _():
                 self.along_x(group, at, 1 - self.x).wait_recv()
                 self.along_y(group, at * self.X + 1 - self.x, True).start()
+                self.across(group, at * self.X + 1 - self.x, True).start()
 
     def others(self):
         count = self.X * self.Z
@@ -142,11 +151,12 @@
     def y_stage(self, group):
         for shard in self.others():
             self.along_y(group, shard, False).wait_recv()
-            self.across(group, shard, True).start()
+            self.across_rest(group, shard, True).start()
 
     def c_stage(self, group):
         for shard in self.others():
             self.across(group, shard, False).wait_recv()
+            self.across_rest(group, shard, False).wait_recv()
 
     def close(self, group):
         for at in range(self.Z):
@@ -163,6 +173,7 @@
         for shard in self.others():
             self.along_y(group, shard, True).wait_send()
             self.across(group, shard, True).wait_send()
+            self.across_rest(group, shard, True).wait_send()
 
 
 def kernel(
@@ -171,7 +182,7 @@
     out_ref, grad_ref,
     weights, x_win, normed, qkv, att, probs, near_probs, streams, cots, normed_t, qkv_t, ga_t, shares_t, score_t,
     rows_a, attn_t, grads, gown, ga_win, tot, tot_got, dlt, dlt_got, acc,
-    load_sem, zs, zr, xs, xr, ys, yr, cs, cr, hs, hr, bs, br, ds, dr, es, er, ts, tr, us, ur,
+    load_sem, zs, zr, xs, xr, ys, yr, cs, cr, ps, pr, hs, hr, bs, br, ds, dr, es, er, ts, tr, us, ur,
 ):
     s = lax.axis_index("space")
     f = lax.axis_index("frame")
@@ -277,7 +288,7 @@
         copy.start()
     for load in loads:
         load.wait()
-    gather = Gather(weights, (zs, zr, xs, xr, ys, yr, cs, cr)) if gathers else None
+    gather = Gather(weights, (zs, zr, xs, xr, ys, yr, cs, cr, ps, pr)) if gathers else None
 
     def pass_on(*steps):
         if gathers:
@@ -535,6 +546,7 @@
             dma((4,)),
             dma((2, 2, 4)), dma((2, 4)), dma((2, 4)), dma((2, 4)),
             dma((2, 8)), dma((2, 8)), dma((2, 8)), dma((2, 8)),
+            dma((2, 8)), dma((2, 8)),
             *[dma((2,))] * 8,
             *[dma((frames - 1,)), dma((frames,))] * 2,
         ],

time: 78.8 us -> 79.1 us (level)
  no operation moved by 1% of the time
where the time goes in v6:
time: 79.1 us; the launch traced here: 78.7 us
  Pallas kernels  74.3 us (94%)
  local copies, waits for them, and re-layouts  3.68 us (5%)
    pallas_call x1, Pallas kernels, local(): pl.pallas_call(functools.partial(kernel, frames, count, gathers), out_sha...  74.3 us
    unnamed x7, local copies, waits for them, and re-layouts  3.68 us

profile of v6, /device:TPU:3, one launch (start us, length us, event | category | flops | bytes accessed | tf_op | source)
XLA Modules:
  0.0 78.7 jit_solution(10993537353793089911)
XLA Ops:
  0.6 0.0 copy-start.1
  0.6 0.7 copy-done.1
  1.3 0.7 copy.9.nb_ref
  2.0 74.3 %shard_map.86 = (bf16[128,768]{1,0:T(8,128)(2,1)}, bf16[128,768]{1,0:T(8,128)(2,1)}) custom-call(bf16[128,768]{1,0:T(8,128)(2,1)} %bitcast.4, bf16[128,768]{1,0:T(8,128)(2,1)} %bitcast.5, bf16[96,2304]{1,0:T(8,128)(2,1)} %wqs_ref.1, bf16[96,768]{1,0:T(8,128)(2,1)} %wos_ref.1, bf16[96,2304]{1,0:T(8,128)(2,1)} %wqt_ref.1, bf16[96,768]{1,0:T(8,128)(2,1)} %wot_ref.1, ...), custom_call_target="tpu_custom_call" | custom-call | tf_op jit(solution)/shard_map/pallas_call | solution.py:522
  76.3 0.0 copy-start
  76.3 1.7 %copy.12 = bf16[1,128,768]{2,1,0:T(8,128)(2,1)} copy(bf16[1,128,768]{2,1,0:T(8,128)(2,1)} %bitcast.7) | data formatting | bytes 393216
  78.0 0.0 copy-done
  78.0 0.7 copy.13
Async XLA Ops:
  0.6 0.7 copy-start.1
  76.3 1.7 %copy-start = (bf16[128,768]{1,0:T(8,128)(2,1)S(1)}, bf16[128,768]{1,0:T(8,128)(2,1)}, u32[]{:S(2)}) copy-start(bf16[128,768]{1,0:T(8,128)(2,1)} %get-tuple-element.5) | copy-start | bytes 589828

commit v7 on v4

--- a/solution.py
+++ b/solution.py
@@ -296,7 +296,7 @@
     forward(normed, 0, 0, D, into(qkv))
     pass_on(("z_step", 1, 3), ("x_step", 1, 1))
     forward(normed, 0, D, 2 * D, into(qkv, D))
-    pass_on(("x_step", 1, 2), ("x_step", 1, 3))
+    pass_on(("x_step", 1, 2))
 
     def listed(block):
         hit = nb_ref[s, 0] == block
@@ -330,6 +330,7 @@
         totals = attend(hp, totals)
     tot[...] = totals.T[:16]
     leave(tot_halo)
+    pass_on(("x_step", 1, 3))
 
     forward(att, 0, 3 * D, D, into(acc))
     streams[mine, :] = (x_ref[...].astype(F32) + acc[...]).astype(BF16)

time: 78.8 us -> 78.8 us (level)
  no operation moved by 1% of the time
where the time goes in v7:
time: 78.8 us; the launch traced here: 78.5 us
  Pallas kernels  74.1 us (94%)
  local copies, waits for them, and re-layouts  3.68 us (5%)
    pallas_call x1, Pallas kernels, local(): pl.pallas_call(functools.partial(kernel, frames, count, gathers), out_sha...  74.1 us
    unnamed x7, local copies, waits for them, and re-layouts  3.68 us

profile of v7, /device:TPU:3, one launch (start us, length us, event | category | flops | bytes accessed | tf_op | source)
XLA Modules:
  0.0 78.5 jit_solution(17688437526915516919)
XLA Ops:
  0.6 0.0 copy-start.1
  0.6 0.7 copy-done.1
  1.3 0.7 copy.9.nb_ref
  2.0 74.1 %shard_map.86 = (bf16[128,768]{1,0:T(8,128)(2,1)}, bf16[128,768]{1,0:T(8,128)(2,1)}) custom-call(bf16[128,768]{1,0:T(8,128)(2,1)} %bitcast.4, bf16[128,768]{1,0:T(8,128)(2,1)} %bitcast.5, bf16[96,2304]{1,0:T(8,128)(2,1)} %wqs_ref.1, bf16[96,768]{1,0:T(8,128)(2,1)} %wos_ref.1, bf16[96,2304]{1,0:T(8,128)(2,1)} %wqt_ref.1, bf16[96,768]{1,0:T(8,128)(2,1)} %wot_ref.1, ...), custom_call_target="tpu_custom_call" | custom-call | tf_op jit(solution)/shard_map/pallas_call | solution.py:512
  76.1 0.0 copy-start
  76.1 1.7 %copy.12 = bf16[1,128,768]{2,1,0:T(8,128)(2,1)} copy(bf16[1,128,768]{2,1,0:T(8,128)(2,1)} %bitcast.7) | data formatting | bytes 393216
  77.8 0.0 copy-done
  77.8 0.7 copy.13
Async XLA Ops:
  0.6 0.7 copy-start.1
  76.1 1.7 %copy-start = (bf16[128,768]{1,0:T(8,128)(2,1)S(1)}, bf16[128,768]{1,0:T(8,128)(2,1)}, u32[]{:S(2)}) copy-start(bf16[128,768]{1,0:T(8,128)(2,1)} %get-tuple-element.5) | copy-start | bytes 589828
